TPU v7x, 128 devices: a whole 4x4x4 slice. The times are simulated.
128 devices in a mesh: dp: 32 (over x, z, core), tensor: 4 (over y).
Axes of the slice: x: 4, y: 4, z: 4, core: 2. Of those that a mesh axis runs over, the one named last changes fastest.
Arguments:
- activations: bfloat16 [3072, 8192], P('dp', 'tensor'), may hold values from -6.5 to 6.5
- targets: bfloat16 [3072, 8192], P('dp', 'tensor'), may hold values from -22 to 22
- key_weight: bfloat16 [8192, 1024], P('dp', 'tensor'), may hold values from -6 to 6
Outputs:
- rotated: float32 [8192, 1024], P('dp', 'tensor')
All inputs are finite; a program needn't handle non-finite values.
Results may differ from a plain program's by a relative error of at most 0.0003.
Values may be sent and summed in bfloat16 or wider, within the bound.
A program may use at most 64 MiB of HBM per device.

v0:
```python
import jax
import jax.numpy as jnp
from jax import lax
from jax.sharding import PartitionSpec as P

ITERS = 2


ridge_weight = 0.5


def local(activations, targets, key_weight):
    n_dp = lax.axis_size("dp")
    n_tensor = lax.axis_size("tensor")
    tok_rows = activations.shape[0]
    token_count = tok_rows * n_dp
    sub_rows = tok_rows // n_tensor
    tensor_place = lax.axis_index("tensor")
    x_full, y_full = (
        lax.all_gather(activations, "tensor", axis=1, tiled=True),
        lax.all_gather(targets, "tensor", axis=1, tiled=True),
    )
    x_sub = lax.dynamic_slice_in_dim(x_full, tensor_place * sub_rows, sub_rows, 0)
    kernel = (
        lax.dot_general(
            x_full,
            lax.all_gather(x_sub, "dp", axis=0, tiled=True),
            (((1,), (1,)), ((), ())),
            preferred_element_type=jnp.float32,
        )
        / token_count
    )
    local_cols = key_weight.shape[1]
    rhs_part = jnp.dot(
        y_full,
        lax.all_gather(key_weight, "dp", axis=0, tiled=True),
        preferred_element_type=jnp.float32,
    )
    rhs = lax.all_gather(rhs_part, "tensor", axis=1, tiled=True)
    dual_state = jnp.zeros_like(rhs)
    residual = rhs

    def square_sum(vector):
        return lax.psum(jnp.sum(vector * vector, axis=0), "dp")

    direction = rhs
    resid_norm = square_sum(residual)
    for step_index in range(ITERS):
        vector_sub = lax.dynamic_slice_in_dim(direction, tensor_place * sub_rows, sub_rows, 0)
        partial_sum = jnp.dot(
            kernel,
            lax.all_gather(vector_sub, "dp", axis=0, tiled=True),
            precision=lax.Precision.HIGHEST,
        )
        applied = lax.psum(partial_sum, "tensor")
        image = applied + ridge_weight * direction
        curve_sum = lax.psum(jnp.sum(direction * image, axis=0), "dp")
        step_alpha = resid_norm / curve_sum
        dual_state = dual_state + step_alpha * direction
        residual = residual - step_alpha * image
        if step_index + 1 < ITERS:
            new_norm = square_sum(residual)
            direction = residual + new_norm / resid_norm * direction
            resid_norm = new_norm
    state_cols = lax.dynamic_slice_in_dim(dual_state, tensor_place * local_cols, local_cols, 1)
    x_slice = x_full.astype(jnp.float32)
    return lax.psum_scatter(
        lax.dot_general(
            x_slice, state_cols, (((0,), (0,)), ((), ())), precision=lax.Precision.HIGHEST
        )
        / token_count,
        "dp",
        scatter_dimension=0,
        tiled=True,
    )


def solution(mesh):
    placed = (P("dp", "tensor"), P("dp", "tensor"), P("dp", "tensor"))
    return jax.shard_map(
        local, mesh=mesh, in_specs=placed, out_specs=P("dp", "tensor"), check_vma=False
    )
```

profile of v0, /device:TPU:1, one launch (start us, length us, event | category | flops | bytes accessed | tf_op | source)
XLA Modules:
  0.0 660.6 jit_solution(10540175944530182857)
XLA Ops:
  6.5 0.0 all-gather.11.cloned.1.call-start
  6.5 0.7 all-gather.11.cloned.1.call-update
  7.3 0.0 all-gather.7.cloned.1.call-start
  7.3 0.7 all-gather.7.cloned.1.call-update
  8.0 0.0 all-gather.9.cloned.1.call-start
  8.1 0.7 all-gather.9.cloned.1.call-update
  8.7 0.0 all-gather.13.cloned.1.call-start
  8.8 30.0 %all-gather.11.cloned.1.call-done = bf16[96,8192]{1,0:T(8,128)(2,1)} async-done(((bf16[96,2048]{1,0:T(8,128)(2,1)}), bf16[96,8192]{1,0:T(8,128)(2,1)}) %all-gather.11.cloned.1.call-update) | async-done | bytes 1572880 | tf_op jit(solution)/shard_map/all_gather | solution.py:20
  38.8 1.8 constant_dynamic-slice_fusion.2
  40.6 0.0 all-gather.13.cloned.1.call-update
  40.6 0.0 copy-start
  40.6 0.0 all-gather.15.cloned.1.call-start
  40.7 26.4 %all-gather.7.cloned.1.call-done = bf16[96,8192]{1,0:T(8,128)(2,1)} async-done(((bf16[96,2048]{1,0:T(8,128)(2,1)}), bf16[96,8192]{1,0:T(8,128)(2,1)}) %all-gather.7.cloned.1.call-update) | async-done | bytes 1572880 | tf_op jit(solution)/shard_map/all_gather | solution.py:21
  67.1 49.2 %all-gather.9.cloned.1.call-done = bf16[8192,256]{1,0:T(8,128)(2,1)} async-done(((bf16[256,256]{1,0:T(8,128)(2,1)}), bf16[8192,256]{1,0:T(8,128)(2,1)}) %all-gather.9.cloned.1.call-update) | async-done | bytes 4194320 | tf_op jit(solution)/shard_map/all_gather | solution.py:36
  116.2 3.5 fusion.6
  119.7 10.7 %all_gather.23 = f32[96,1024]{1,0:T(8,128)S(1)} all-gather(f32[96,256]{1,0:T(8,128)S(1)} %fusion.6), channel_id=1, replica_groups=mesh['dp'=32,'tensor'=4] {'tensor'}, dimensions={1}, use_global_device_ids=true | all-gather | bytes 491520 | tf_op jit(solution)/shard_map/all_gather | solution.py:39
  130.4 0.6 constant_dynamic-slice_fusion.1
  131.1 0.0 all-gather.15.cloned.1.call-update
  131.1 0.0 all-reduce.4.cloned.1.call-start
  131.1 49.5 %all-gather.13.cloned.1.call-done = bf16[768,8192]{1,0:T(8,128)(2,1)} async-done(((bf16[24,8192]{1,0:T(8,128)(2,1)}), bf16[768,8192]{1,0:T(8,128)(2,1)}) %all-gather.13.cloned.1.call-update) | async-done | bytes 12582928 | tf_op jit(solution)/shard_map/all_gather | solution.py:27
  180.7 0.0 copy-done
  180.7 8.6 %convolution_multiply_fusion.1 = f32[768,96]{0,1:T(8,128)S(1)} fusion(bf16[768,8192]{1,0:T(8,128)(2,1)} %all-gather.13.cloned.1.call-done, bf16[96,8192]{1,0:T(8,128)(2,1)S(1)} %copy-done), kind=kOutput, calls=%fused_computation.2 | convolution fusion | flops 1208033280 | bytes 14450688 | tf_op jit(solution)/shard_map/dot_general | solution.py:25
  189.2 38.2 %all-gather.15.cloned.1.call-done = f32[768,1024]{1,0:T(8,128)} async-done(((f32[24,1024]{1,0:T(8,128)}), f32[768,1024]{1,0:T(8,128)}) %all-gather.15.cloned.1.call-update) | async-done | bytes 3145744 | tf_op jit(solution)/shard_map/all_gather | solution.py:52
  227.4 4.6 fusion.7
  232.0 0.0 all-reduce.4.cloned.1.call-update
  232.0 0.0 all-gather.17.cloned.1.call-start
  232.0 39.0 %all-reduce.4.cloned.1.call-done = f32[96,1024]{1,0:T(8,128)} async-done(((f32[96,1024]{1,0:T(8,128)}), f32[96,1024]{1,0:T(8,128)}) %all-reduce.4.cloned.1.call-update) | async-done | bytes 393232 | tf_op jit(solution)/shard_map/psum | solution.py:55
  271.1 1.1 multiply_reduce_fusion.2
  272.2 66.0 %all-reduce = (f32[1024]{0:T(1024)S(1)}, f32[1024]{0:T(1024)S(1)}) all-reduce(f32[1024]{0:T(1024)S(1)} %get-tuple-element.6, f32[1024]{0:T(1024)S(1)} %get-tuple-element.5), channel_id=1, replica_groups=mesh['dp'=32,'tensor'=4] {'dp'}, use_global_device_ids=true, to_apply=%region_1.0 | all-reduce | flops 2048 | bytes 16384 | tf_op jit(solution)/shard_map/psum | solution.py:44
  338.1 1.1 multiply_reduce_fusion.1
  339.2 65.0 %psum.45 = f32[1024]{0:T(1024)S(1)} all-reduce(f32[1024]{0:T(1024)S(1)} %multiply_reduce_fusion.1), channel_id=1, replica_groups=mesh['dp'=32,'tensor'=4] {'dp'}, use_global_device_ids=true, to_apply=%region_6.0 | all-reduce | flops 1024 | bytes 8192 | tf_op jit(solution)/shard_map/psum | solution.py:44
  404.2 1.1 multiply_add_fusion
  405.3 0.7 constant_dynamic-slice_fusion
  405.9 0.0 all-gather.17.cloned.1.call-update
  406.0 0.0 all-reduce.6.cloned.1.call-start
  406.0 41.4 %all-gather.17.cloned.1.call-done = f32[768,1024]{1,0:T(8,128)} async-done(((f32[24,1024]{1,0:T(8,128)}), f32[768,1024]{1,0:T(8,128)}) %all-gather.17.cloned.1.call-update) | async-done | bytes 3145744 | tf_op jit(solution)/shard_map/all_gather | solution.py:52
  447.4 4.6 fusion.8
  452.0 0.0 all-reduce.6.cloned.1.call-update
  452.0 0.0 reduce-scatter.2.cloned.1.call-start
  452.0 0.1 dynamic-slice
  452.1 38.9 %all-reduce.6.cloned.1.call-done = f32[96,1024]{1,0:T(8,128)} async-done(((f32[96,1024]{1,0:T(8,128)}), f32[96,1024]{1,0:T(8,128)}) %all-reduce.6.cloned.1.call-update) | async-done | bytes 393232 | tf_op jit(solution)/shard_map/psum | solution.py:55
  491.1 1.1 multiply_reduce_fusion
  492.1 65.0 %psum.47 = f32[1024]{0:T(1024)S(1)} all-reduce(f32[1024]{0:T(1024)S(1)} %multiply_reduce_fusion), channel_id=1, replica_groups=mesh['dp'=32,'tensor'=4] {'dp'}, use_global_device_ids=true, to_apply=%region_9.0 | all-reduce | flops 1024 | bytes 8192 | tf_op jit(solution)/shard_map/psum | solution.py:57
  557.1 0.1 dynamic-slice.1
  557.2 5.9 fusion
  563.1 0.0 reduce-scatter.2.cloned.1.call-update
  563.1 89.2 %reduce-scatter.2.cloned.1.call-done = f32[256,256]{0,1:T(8,128)} async-done(((f32[8192,256]{0,1:T(8,128)}), f32[256,256]{0,1:T(8,128)}) %reduce-scatter.2.cloned.1.call-update) | async-done | bytes 262160 | tf_op jit(solution)/shard_map/reduce_scatter | solution.py:67
  652.3 1.8 copy.4
  (3 shorter events, 0.0 us)
Async XLA Ops:
  6.5 32.3 %all-gather.11.cloned.1.call-start = ((), (), s32[]{:S(2)}) async-start(), calls=%async_computation.3 | async-start | bytes 1966080 | tf_op jit(solution)/shard_map/all_gather | solution.py:20
  7.3 59.8 %all-gather.7.cloned.1.call-start = ((), (), s32[]{:S(2)}) async-start(), calls=%async_computation.1 | async-start | bytes 1966080 | tf_op jit(solution)/shard_map/all_gather | solution.py:21
  8.0 108.2 %all-gather.9.cloned.1.call-start = ((), (), s32[]{:S(2)}) async-start(), calls=%async_computation.2 | async-start | bytes 4325376 | tf_op jit(solution)/shard_map/all_gather | solution.py:36
  8.7 171.9 %all-gather.13.cloned.1.call-start = ((), (), s32[]{:S(2)}) async-start(), calls=%async_computation.4 | async-start | bytes 12976128 | tf_op jit(solution)/shard_map/all_gather | solution.py:27
  40.6 140.1 %copy-start = (bf16[96,8192]{1,0:T(8,128)(2,1)S(1)}, bf16[96,8192]{1,0:T(8,128)(2,1)}, u32[]{:S(2)}) copy-start(bf16[96,8192]{1,0:T(8,128)(2,1)} %all-gather.11.cloned.1.call-done) | copy-start | bytes 4718596
  40.6 186.8 %all-gather.15.cloned.1.call-start = ((), (), s32[]{:S(2)}) async-start(), calls=%async_computation.5 | async-start | bytes 3244032 | tf_op jit(solution)/shard_map/all_gather | solution.py:52
  131.1 140.0 %all-reduce.4.cloned.1.call-start = ((), (), s32[]{:S(2)}) async-start(), calls=%async_computation.6 | async-start | bytes 786432 | tf_op jit(solution)/shard_map/psum | solution.py:55
  232.0 215.4 %all-gather.17.cloned.1.call-start = ((), (), s32[]{:S(2)}) async-start(), calls=%async_computation.7 | async-start | bytes 3244032 | tf_op jit(solution)/shard_map/all_gather | solution.py:52
  406.0 85.1 %all-reduce.6.cloned.1.call-start = ((), (), s32[]{:S(2)}) async-start(), calls=%async_computation.8 | async-start | bytes 786432 | tf_op jit(solution)/shard_map/psum | solution.py:55
  452.0 200.3 %reduce-scatter.2.cloned.1.call-start = ((), (), s32[]{:S(2)}) async-start(), calls=%async_computation.9 | async-start | bytes 8650752 | tf_op jit(solution)/shard_map/reduce_scatter | solution.py:67
Sparse Core Ops, SparseCore 0:
  9.0 29.7 all-gather.10
  40.5 26.5 all-gather.6
  69.4 46.8 all-gather.8
  118.4 62.2 all-gather.12
  182.8 44.6 all-gather.14
  232.1 38.9 all-reduce.3
  406.1 41.2 all-gather.16
  452.1 38.8 all-reduce.5
  563.3 88.9 reduce-scatter.1
where the time goes:
time: 662 us; the launch traced here: 661 us
  waiting for transfers between devices  404 us (61%)
  blocking collectives  207 us (31%)
  matrix products  27.1 us (4%)
  between operations  13.3 us (2%)
    psum x2, blocking collectives, square_sum(): return lax.psum(jnp.sum(vector * vector, axis=0), 'dp')  131 us
    reduce_scatter x1, waiting for transfers between devices, local(): lax.psum_scatter(lax.dot_general(x_slice, state_cols, (((0,), (0,)), ((),...  89.2 us
    all_gather x2, waiting for transfers between devices, local(): lax.all_gather(vector_sub, 'dp', axis=0, tiled=True)  79.5 us
    psum x2, waiting for transfers between devices, local(): applied = lax.psum(partial_sum, 'tensor')  78 us
    psum x1, blocking collectives, local(): curve_sum = lax.psum(jnp.sum(direction * image, axis=0), 'dp')  65 us
    all_gather x1, waiting for transfers between devices, local(): lax.all_gather(x_sub, 'dp', axis=0, tiled=True)  49.5 us
    all_gather x1, waiting for transfers between devices, local(): lax.all_gather(key_weight, 'dp', axis=0, tiled=True)  49.2 us
    all_gather x1, waiting for transfers between devices, local(): lax.all_gather(activations, 'tensor', axis=1, tiled=True)  30 us
  transfers between devices with their start and end apart: 9, of which 9 were waited for; matrix products, arithmetic and copies ran while one was open for 2% of the time, Pallas kernels for 0%

commit v1 on v0

v1 whole, which is shorter than its diff:
```python
import jax
import jax.numpy as jnp
from jax import lax
from jax.experimental import pallas as pl
from jax.experimental.pallas import tpu as pltpu
from jax.sharding import PartitionSpec as P

MESH = pl.DeviceIdType.MESH
TOKENS = 3072
RIDGE = 0.5
F32, BF16 = jnp.float32, jnp.bfloat16


def device(x, y, z, c):
    return (x * 8 + z * 2 + c, y)


def split(value):
    high = value.astype(BF16)
    return high, (value - high.astype(F32)).astype(BF16)


class Copies:
    def __init__(self, send, recv):
        self.send, self.recv, self.started = send, recv, []

    def start(self, index, src, dst, target):
        copy = pltpu.make_async_remote_copy(
            src_ref=src,
            dst_ref=dst,
            send_sem=self.send.at[index],
            recv_sem=self.recv.at[index],
            device_id=target,
            device_id_type=MESH,
        )
        copy.start()
        self.started.append(copy)

    def arrived(self, index, dst, source):
        pltpu.make_async_remote_copy(
            src_ref=dst,
            dst_ref=dst,
            send_sem=self.send.at[index],
            recv_sem=self.recv.at[index],
            device_id=source,
            device_id_type=MESH,
        ).wait_recv()

    def finish(self):
        for copy in self.started:
            copy.wait_send()


def kernel(
    x_ref, y_ref, w_ref, out_ref,
    y_sort, y_all, w_all, x_mine, x_all, x_full, x_flip,
    b_part, b_other, b_all, b_pair, u0, u_pair, ud,
    v_part, v_in1, v_sum, v_in2, v_all, r_all, gamma, o_mine, o_in,
    y_s, y_r, w_s, w_r, x_s, x_r, xy_s, xy_r, xc_s, xc_r, p_s, p_r,
    b_s, b_r, v_s, v_r, g_s, g_r, o_s, o_r,
):
    i = lax.axis_index("dp")
    y = lax.axis_index("tensor")
    x, z, c = i // 8, lax.rem(i // 2, 4), lax.rem(i, 2)
    mine = x * 4 + z
    twin = 1 - c

    def at(a, d):
        return lax.rem(a + d, 4)

    barrier = pltpu.get_barrier_semaphore()
    partners = [(dx, dz) for dx in range(4) for dz in range(4) if dx or dz]
    peers = [device(at(x, dx), y, at(z, dz), c) for dx, dz in partners]
    peers += [device(x, at(y, d), z, e) for d in range(1, 4) for e in (c, twin)]
    peers += [device(x, y, z, twin)]
    slot = lax.rem(z, 2) * 2 + c
    owner = z // 2
    stays = jnp.logical_and(x == z, owner == c)
    for k in range(4):

        @pl.when(jnp.logical_not(jnp.logical_and(stays, slot == k)))
        def _():
            pl.semaphore_signal(barrier, inc=1, device_id=device(z, y, 2 * c + k // 2, k % 2), device_id_type=MESH)

    for peer in peers:
        pl.semaphore_signal(barrier, inc=1, device_id=peer, device_id_type=MESH)

    for e in range(2):
        for h in range(2):
            for q in range(4):
                y_sort[e, :, h * 512 + q * 128 : h * 512 + q * 128 + 128] = y_ref[
                    :, q * 512 + e * 256 + h * 128 : q * 512 + e * 256 + h * 128 + 128
                ]
    for h in range(2):
        w_all[h, mine] = w_ref[h * 128 : h * 128 + 128, :]
    pl.semaphore_wait(barrier, len(peers) + 4 - stays.astype(jnp.int32))

    wc = Copies(w_s, w_r)
    yc = Copies(y_s, y_r)
    xc = Copies(x_s, x_r)
    bc = Copies(b_s, b_r)
    vc = Copies(v_s, v_r)

    def gather_first(copies, buf):
        for d in range(1, 4):
            copies.start(d - 1, buf.at[0, mine], buf.at[0, mine], device(at(x, d), y, z, c))
            copies.start(d + 2, buf.at[1, mine], buf.at[1, mine], device(x, y, at(z, d), c))

    def forward(copies, buf, j):
        block0 = at(x, 4 - j) * 4 + z
        block1 = x * 4 + at(z, 4 - j)
        if j:
            copies.arrived(j - 1, buf.at[0, block0], device(at(x, 4 - j), y, z, c))
        for d in range(1, 4):
            copies.start(6 + j * 3 + d - 1, buf.at[0, block0], buf.at[0, block0], device(x, y, at(z, d), c))
        if j:
            copies.arrived(j + 2, buf.at[1, block1], device(x, y, at(z, 4 - j), c))
        for d in range(1, 4):
            copies.start(18 + j * 3 + d - 1, buf.at[1, block1], buf.at[1, block1], device(at(x, d), y, z, c))

    def gather_last(copies, buf):
        for j in range(4):
            for d in range(1, 4):
                block0 = at(x, 4 - j) * 4 + at(z, 4 - d)
                copies.arrived(6 + j * 3 + d - 1, buf.at[0, block0], device(x, y, at(z, 4 - d), c))
                block1 = at(x, 4 - d) * 4 + at(z, 4 - j)
                copies.arrived(18 + j * 3 + d - 1, buf.at[1, block1], device(at(x, 4 - d), y, z, c))

    gather_first(wc, w_all)
    for d in range(4):
        for e in range(2):
            if d or e:
                target = lax.rem(c + e, 2)
                yc.start(d * 2 + e, y_sort.at[target], y_all.at[y, c], device(x, at(y, d), z, target))
    y_all[y, c] = y_sort[c]
    for k, (dx, dz) in enumerate(partners):
        block = at(x, dx) * 4 + at(z, dz)
        columns = pl.ds(pl.multiple_of(block * 128, 128), 128)
        xc.start(k, x_ref.at[:, columns], x_mine.at[mine], device(at(x, dx), y, at(z, dz), c))
    x_mine[mine] = x_ref[:, pl.ds(pl.multiple_of(mine * 128, 128), 128)]

    for j in (0, 1, 3, 2):
        forward(wc, w_all, j)
    for k, (dx, dz) in enumerate(partners):
        sx, sz = at(x, 4 - dx), at(z, 4 - dz)
        xc.arrived(k, x_mine.at[sx * 4 + sz], device(sx, y, sz, c))
    for d in range(4):
        for e in range(2):
            if d or e:
                source = lax.rem(c + e, 2)
                yc.arrived(d * 2 + e, y_all.at[at(y, 4 - d), source], device(x, at(y, 4 - d), z, source))

    xyc = Copies(xy_s, xy_r)
    xcc = Copies(xc_s, xc_r)
    for d in range(1, 4):
        xyc.start(d - 1, x_mine, x_all.at[y, c], device(x, at(y, d), z, c))
    xcc.start(0, x_mine, x_all.at[y, c], device(x, y, z, twin))
    x_all[y, c] = x_mine[...]
    gather_last(wc, w_all)

    part = jnp.zeros((192, 256), F32)
    for s in range(4):
        for h in range(2):
            part += jnp.dot(
                y_all[s, :, :, h * 512 : h * 512 + 512].reshape(192, 512),
                w_all[h, 4 * s : 4 * s + 4].reshape(512, 256),
                preferred_element_type=F32,
            )
    b_part[0] = part[:, :128]
    b_part[1] = part[:, 128:]
    pc = Copies(p_s, p_r)
    pc.start(0, b_part.at[twin], b_other, device(x, y, z, twin))
    pc.arrived(0, b_other, device(x, y, z, twin))
    for h in range(2):
        b_all[h, mine] = b_part[c, h * 96 : h * 96 + 96] + b_other[h * 96 : h * 96 + 96]
    gather_first(bc, b_all)
    for j in (0, 1, 3, 2):
        forward(bc, b_all, j)

    for d in range(1, 4):
        source = at(y, 4 - d)
        xyc.arrived(d - 1, x_all.at[source, c], device(x, source, z, c))
        xcc.start(d, x_all.at[source, c], x_all.at[source, c], device(x, y, z, twin))
    for d in range(4):
        source = at(y, 4 - d)
        xcc.arrived(d, x_all.at[source, twin], device(x, y, z, twin))

    for s in range(4):
        for e in range(2):
            piece = x_all[s, e].reshape(1536, 128)
            x_full[e * 1536 : e * 1536 + 1536, s * 128 : s * 128 + 128] = piece
            x_flip[s * 128 : s * 128 + 128, e * 1536 : e * 1536 + 1536] = piece.T

    gather_last(bc, b_all)
    bb = jnp.zeros((1, 128), F32)
    for h in range(2):
        value = b_all[h].reshape(1536, 128)
        bb += jnp.sum(value * value, axis=0, keepdims=True)
        high, low = split(value)
        b_pair[h * 1536 : h * 1536 + 1536, :128] = high
        b_pair[h * 1536 : h * 1536 + 1536, 128:] = low
    wide = jnp.dot(x_flip[...], b_pair[...], preferred_element_type=F32)
    first = wide[:, :128] + wide[:, 128:]
    u0[...] = first
    high, low = split(first * (1.0 / TOKENS))
    u_pair[:, :128] = high
    u_pair[:, 128:] = low

    def block_of(h, place):
        rows = pl.ds(pl.multiple_of(h * 1536 + place * 384, 128), 384)
        wide = jnp.dot(x_full[rows, :], u_pair[...], preferred_element_type=F32)
        v_part[h, place] = (wide[:, :128] + wide[:, 128:]).reshape(4, 96, 128)

    for d in (1, 3, 2):
        block_of(0, at(x, d))
        vc.start(36 + d - 1, v_part.at[0, at(x, d)], v_in1.at[0, d - 1], device(at(x, d), y, z, c))
    for place in range(4):
        block_of(1, place)
    for d in (1, 3, 2):
        vc.start(39 + d - 1, v_part.at[1, :, at(z, d)], v_in1.at[1, d - 1], device(x, y, at(z, d), c))
    block_of(0, x)
    for d in (1, 3, 2):
        vc.arrived(36 + d - 1, v_in1.at[0, d - 1], device(at(x, 4 - d), y, z, c))
    v_sum[0] = v_part[0, x] + v_in1[0, 0] + v_in1[0, 1] + v_in1[0, 2]
    for d in (1, 3, 2):
        vc.start(30 + d - 1, v_sum.at[0, at(z, d)], v_in2.at[0, d - 1], device(x, y, at(z, d), c))
    for d in (1, 3, 2):
        vc.arrived(39 + d - 1, v_in1.at[1, d - 1], device(x, y, at(z, 4 - d), c))
    v_sum[1] = v_part[1, :, z] + v_in1[1, 0] + v_in1[1, 1] + v_in1[1, 2]
    for d in (1, 3, 2):
        vc.start(33 + d - 1, v_sum.at[1, at(x, d)], v_in2.at[1, d - 1], device(at(x, d), y, z, c))
    for d in (1, 3, 2):
        vc.arrived(30 + d - 1, v_in2.at[0, d - 1], device(x, y, at(z, 4 - d), c))
    v_all[0, mine] = v_sum[0, z] + v_in2[0, 0] + v_in2[0, 1] + v_in2[0, 2]
    for d in (1, 3, 2):
        vc.arrived(33 + d - 1, v_in2.at[1, d - 1], device(at(x, 4 - d), y, z, c))
    v_all[1, mine] = v_sum[1, x] + v_in2[1, 0] + v_in2[1, 1] + v_in2[1, 2]
    gather_first(vc, v_all)
    for j in (0, 1, 3, 2):
        forward(vc, v_all, j)
    gather_last(vc, v_all)

    bv = jnp.zeros((1, 128), F32)
    for h in range(2):
        bv += jnp.sum((b_all[h] * v_all[h]).reshape(1536, 128), axis=0, keepdims=True)
    alpha = bb / (bv + RIDGE * bb)
    norm = jnp.zeros((1, 128), F32)
    for h in range(2):
        value = b_all[h].reshape(1536, 128)
        residual = value - alpha * (v_all[h].reshape(1536, 128) + RIDGE * value)
        norm += jnp.sum(residual * residual, axis=0, keepdims=True)
        r_all[h] = residual
        high, low = split(residual)
        b_pair[h * 1536 : h * 1536 + 1536, :128] = high
        b_pair[h * 1536 : h * 1536 + 1536, 128:] = low
    beta = norm / bb
    wide = jnp.dot(x_flip[...], b_pair[...], preferred_element_type=F32)
    turned = wide[:, :128] + wide[:, 128:] + beta * u0[...]
    ud[...] = turned
    gamma[mine] = jnp.broadcast_to(jnp.sum(turned * turned, axis=0, keepdims=True), (8, 128))
    gc = Copies(g_s, g_r)
    for k, (dx, dz) in enumerate(partners):
        gc.start(k, gamma.at[mine], gamma.at[mine], device(at(x, dx), y, at(z, dz), c))
    dd = jnp.zeros((1, 128), F32)
    for h in range(2):
        turn = r_all[h] + beta * b_all[h].reshape(1536, 128)
        dd += jnp.sum(turn * turn, axis=0, keepdims=True)
    for k, (dx, dz) in enumerate(partners):
        sx, sz = at(x, 4 - dx), at(z, 4 - dz)
        gc.arrived(k, gamma.at[sx * 4 + sz], device(sx, y, sz, c))
    curve = jnp.sum(gamma[...], axis=0)[:1] * (1.0 / TOKENS) + RIDGE * dd
    step = norm / curve
    result = (alpha * u0[...] + step * ud[...]) * (1.0 / TOKENS)
    o_mine[...] = result.reshape(4, 128, 128)

    for p in range(4):
        place = at(x, p)

        def move(place=place):
            return pltpu.make_async_remote_copy(
                src_ref=o_mine.at[place], dst_ref=o_in.at[slot], send_sem=o_s.at[p], recv_sem=o_r.at[slot],
                device_id=device(place, y, x, owner), device_id_type=MESH,
            )

        if p:
            move().start()
        else:

            @pl.when(jnp.logical_not(stays))
            def _():
                move().start()

            @pl.when(stays)
            def _():
                pltpu.make_async_copy(o_mine.at[place], o_in.at[slot], o_r.at[slot]).start()

    for k in range(4):
        pltpu.make_async_copy(o_in.at[k], o_in.at[k], o_r.at[k]).wait()
        t, e = k // 2, k % 2
        out_ref[t * 128 : t * 128 + 128, e * 128 : e * 128 + 128] = o_in[k]
    for p in range(1, 4):
        pltpu.make_async_copy(o_mine.at[p], o_mine.at[p], o_s.at[p]).wait()

    @pl.when(jnp.logical_not(stays))
    def _():
        pltpu.make_async_copy(o_mine.at[0], o_mine.at[0], o_s.at[0]).wait()

    for copies in (wc, yc, xc, bc, vc, xyc, xcc, pc, gc):
        copies.finish()


def local(activations, targets, key_weight):
    vmem = pl.BlockSpec(memory_space=pltpu.VMEM)
    dma = pltpu.SemaphoreType.DMA
    sizes = (8, 30, 15, 3, 4, 1, 30, 42, 15, 4)
    buffers = [
        ((2, 96, 1024), BF16),
        ((4, 2, 96, 1024), BF16),
        ((2, 16, 128, 256), BF16),
        ((16, 96, 128), BF16),
        ((4, 2, 16, 96, 128), BF16),
        ((TOKENS, 512), BF16),
        ((512, TOKENS), BF16),
        ((2, 192, 128), F32),
        ((192, 128), F32),
        ((2, 16, 96, 128), F32),
        ((TOKENS, 256), BF16),
        ((512, 128), F32),
        ((512, 256), BF16),
        ((512, 128), F32),
        ((2, 4, 4, 96, 128), F32),
        ((2, 3, 4, 96, 128), F32),
        ((2, 4, 96, 128), F32),
        ((2, 3, 96, 128), F32),
        ((2, 16, 96, 128), F32),
        ((2, 1536, 128), F32),
        ((16, 8, 128), F32),
        ((4, 128, 128), F32),
        ((4, 128, 128), F32),
    ]
    return pl.pallas_call(
        kernel,
        out_shape=jax.ShapeDtypeStruct((256, 256), F32),
        in_specs=[vmem] * 3,
        out_specs=vmem,
        scratch_shapes=[pltpu.VMEM(*b) for b in buffers] + [dma((n,)) for n in sizes for _ in range(2)],
        compiler_params=pltpu.CompilerParams(collective_id=0, has_side_effects=True, vmem_limit_bytes=48 * 2**20),
    )(activations, targets, key_weight)


def solution(mesh):
    placed = (P("dp", "tensor"), P("dp", "tensor"), P("dp", "tensor"))
    return jax.shard_map(local, mesh=mesh, in_specs=placed, out_specs=P("dp", "tensor"), check_vma=False)
```

time: 662 us -> 99.4 us (0.15)
  waiting for transfers between devices: 404 us -> 0 us
  blocking collectives: 207 us -> 0 us
  Pallas kernels: 0 us -> 95.6 us
  matrix products: 27.1 us -> 0 us
  between operations: 13.3 us -> 0.01 us
    all_gather x6 -> x0, waiting for transfers between devices: 235 us -> none  [the longest x2 79.5 us: local(): lax.all_gather(vector_sub, 'dp', axis=0, tiled=True)]
    psum x3 -> x0, blocking collectives: 196 us -> none  [the longest x2 131 us: square_sum(): return lax.psum(jnp.sum(vector * vector, axis=0), 'dp')]
    pallas_call x0 -> x1, Pallas kernels: none -> 95.6 us  [local(): pl.pallas_call(kernel, out_shape=jax.ShapeDtypeStruct((256, 256), F32), i...]
    reduce_scatter x1 -> x0, waiting for transfers between devices: 89.2 us -> none  [local(): lax.psum_scatter(lax.dot_general(x_slice, state_cols, (((0,), (0,)), ((),...]
    psum x2 -> x0, waiting for transfers between devices: 78 us -> none  [local(): applied = lax.psum(partial_sum, 'tensor')]
    dot_general x5 -> x0, matrix products: 27.1 us -> none  [the longest x2 9.14 us: local(): jnp.dot(kernel, lax.all_gather(vector_sub, 'dp', axis=0, tiled=True), pre...]
    all_gather x1 -> x0, blocking collectives: 10.7 us -> none  [local(): rhs = lax.all_gather(rhs_part, 'tensor', axis=1, tiled=True)]
  transfers between devices with their start and end apart: 9 -> 0, of which waited for: 9 -> 0; matrix products, arithmetic and copies ran while one was open for 2% -> 0% of each run, Pallas kernels for 0% -> 0%
where the time goes in v1:
time: 99.4 us; the launch traced here: 99.2 us
  Pallas kernels  95.6 us (96%)
  local copies, waits for them, and re-layouts  3.6 us (4%)
    pallas_call x1, Pallas kernels, local(): pl.pallas_call(kernel, out_shape=jax.ShapeDtypeStruct((256, 256), F32), i...  95.6 us
    unnamed x7, local copies, waits for them, and re-layouts  3.6 us

profile of v1, /device:TPU:1, one launch (start us, length us, event | category | flops | bytes accessed | tf_op | source)
XLA Modules:
  0.0 99.2 jit_solution(10652075528851766128)
XLA Ops:
  0.0 0.0 copy-start
  0.0 1.0 %copy-done = bf16[96,2048]{1,0:T(8,128)(2,1)S(1)} copy-done((bf16[96,2048]{1,0:T(8,128)(2,1)S(1)}, bf16[96,2048]{1,0:T(8,128)(2,1)}, u32[]{:S(2)}) %copy-start) | copy-done | bytes 393240
  1.0 0.0 copy-start.1
  1.0 1.0 %copy-done.1 = bf16[96,2048]{1,0:T(8,128)(2,1)S(1)} copy-done((bf16[96,2048]{1,0:T(8,128)(2,1)S(1)}, bf16[96,2048]{1,0:T(8,128)(2,1)}, u32[]{:S(2)}) %copy-start.1) | copy-done | bytes 393240
  2.0 0.0 copy-start.2
  2.0 0.9 copy-done.2
  2.9 95.6 %shard_map.37 = f32[256,256]{1,0:T(8,128)S(1)} custom-call(bf16[96,2048]{1,0:T(8,128)(2,1)S(1)} %copy-done, bf16[96,2048]{1,0:T(8,128)(2,1)S(1)} %copy-done.1, bf16[256,256]{1,0:T(8,128)(2,1)S(1)} %copy-done.2), custom_call_target="tpu_custom_call" | custom-call | tf_op jit(solution)/shard_map/pallas_call | solution.py:341
  98.5 0.7 copy.5
Async XLA Ops:
  0.0 1.0 %copy-start = (bf16[96,2048]{1,0:T(8,128)(2,1)S(1)}, bf16[96,2048]{1,0:T(8,128)(2,1)}, u32[]{:S(2)}) copy-start(bf16[96,2048]{1,0:T(8,128)(2,1)} %x_ref.1) | copy-start | bytes 1179652
  1.0 1.0 %copy-start.1 = (bf16[96,2048]{1,0:T(8,128)(2,1)S(1)}, bf16[96,2048]{1,0:T(8,128)(2,1)}, u32[]{:S(2)}) copy-start(bf16[96,2048]{1,0:T(8,128)(2,1)} %y_ref.1) | copy-start | bytes 1179652
  2.0 0.9 copy-start.2

commit v2 on v1

v2 whole, which is shorter than its diff:
```python
import jax
import jax.numpy as jnp
from jax import lax
from jax.experimental import pallas as pl
from jax.experimental.pallas import tpu as pltpu
from jax.sharding import PartitionSpec as P

MESH = pl.DeviceIdType.MESH
TOKENS = 3072
RIDGE = 0.5
F32, BF16 = jnp.float32, jnp.bfloat16


def device(x, y, z, c):
    return (x * 8 + z * 2 + c, y)


def split(value):
    high = value.astype(BF16)
    return high, (value - high.astype(F32)).astype(BF16)


class Copies:
    def __init__(self, send, recv):
        self.send, self.recv, self.started = send, recv, []

    def start(self, index, src, dst, target, lands=None):
        copy = pltpu.make_async_remote_copy(
            src_ref=src,
            dst_ref=dst,
            send_sem=self.send.at[index],
            recv_sem=self.recv.at[index if lands is None else lands],
            device_id=target,
            device_id_type=MESH,
        )
        copy.start()
        self.started.append(copy)

    def arrived(self, index, dst):
        pltpu.make_async_copy(dst, dst, self.recv.at[index]).wait()

    def finish(self):
        for copy in self.started:
            copy.wait_send()


def kernel(
    x_in, y_in, w_in, out_ref,
    x_sort, y_sort, y_all, w_all, x_mine, x_all, x_full, x_flip,
    b_part, b_other, b_all, b_pair, u0, u_pair, ud,
    v_part, v_far, v_merge, v_near, v_sum, v_light, v_all, r_all, gamma, scalars, u_in, d_in,
    l_s, y_s, y_r, w_s, w_r, x_s, x_r, xy_s, xy_r, xc_s, xc_r, p_s, p_r,
    b_s, b_r, v_s, v_r, g_s, g_r, t_s, t_r, u_s, u_r, d_s, d_r,
):
    i = lax.axis_index("dp")
    y = lax.axis_index("tensor")
    x, z, c = i // 8, lax.rem(i // 2, 4), lax.rem(i, 2)
    mine = x * 4 + z
    twin = 1 - c

    def at(a, d):
        return lax.rem(a + d + 4, 4)

    partners = [(dx, dz) for dx in range(4) for dz in range(4) if dx or dz]
    up, down = at(y, 1), at(y, -1)

    slot = lax.rem(z, 2) * 2 + c
    owner = z // 2
    stays = jnp.logical_and(x == z, owner == c)
    barrier = pltpu.get_barrier_semaphore()
    peers = [device(at(x, dx), y, at(z, dz), c) for dx, dz in partners]
    peers += [device(x, place, z, e) for place in (up, down) for e in (c, twin)]
    peers += [device(x, y, z, twin)]
    for peer in peers:
        pl.semaphore_signal(barrier, inc=1, device_id=peer, device_id_type=MESH)
    for k in range(4):

        @pl.when(jnp.logical_not(jnp.logical_and(stays, slot == k)))
        def _():
            pl.semaphore_signal(barrier, inc=1, device_id=device(z, y, 2 * c + k // 2, k % 2), device_id_type=MESH)

    loads = []
    for h in range(2):
        loads.append((w_in.at[h * 128 : h * 128 + 128, :], w_all.at[h, mine]))
    for e in range(2):
        for h in range(2):
            for q in range(4):
                columns = slice(q * 512 + e * 256 + h * 128, q * 512 + e * 256 + h * 128 + 128)
                loads.append((y_in.at[:, columns], y_sort.at[e, :, h * 512 + q * 128 : h * 512 + q * 128 + 128]))
    for k in range(16):
        loads.append((x_in.at[:, k * 128 : k * 128 + 128], x_sort.at[k]))
    loads = [pltpu.make_async_copy(src, dst, l_s.at[k]) for k, (src, dst) in enumerate(loads)]
    for load in loads:
        load.start()
    for load in loads:
        load.wait()
    pl.semaphore_wait(barrier, len(peers) + 4 - stays.astype(jnp.int32))

    wc, yc, xc, xyc, xcc = Copies(w_s, w_r), Copies(y_s, y_r), Copies(x_s, x_r), Copies(xy_s, xy_r), Copies(xc_s, xc_r)
    pc, bc, vc = Copies(p_s, p_r), Copies(b_s, b_r), Copies(v_s, v_r)
    gc, tc, uc, dc = Copies(g_s, g_r), Copies(t_s, t_r), Copies(u_s, u_r), Copies(d_s, d_r)

    def light(h, d):
        return device(at(x, d), y, z, c) if h == 0 else device(x, y, at(z, d), c)

    def heavy(h, d):
        return device(x, y, at(z, d), c) if h == 0 else device(at(x, d), y, z, c)

    def block(h, dl, dh):
        return at(x, dl) * 4 + at(z, dh) if h == 0 else at(x, dh) * 4 + at(z, dl)

    def ring_first(copies, buf):
        for d in (1, 3, 2):
            for h in range(2):
                copies.start(h * 3 + d - 1, buf.at[h, mine], buf.at[h, mine], light(h, d))
        ring_heavy(copies, buf, 0)

    def ring_heavy(copies, buf, j):
        for h in range(2):
            part = buf.at[h, block(h, -j, 0)]
            if j:
                copies.arrived(h * 3 + j - 1, part)
            copies.start(6 + h * 8 + j * 2, part, part, heavy(h, 1))
            copies.start(6 + h * 8 + j * 2 + 1, part, part, heavy(h, -1))

    def ring_forward(copies, buf, j):
        for h in range(2):
            if j in (0, 1):
                part = buf.at[h, block(h, -j, -1)]
                copies.arrived(6 + h * 8 + j * 2, part)
                copies.start(22 + h * 4 + j, part, part, heavy(h, 1))
            else:
                part = buf.at[h, block(h, -j, 1)]
                copies.arrived(6 + h * 8 + j * 2 + 1, part)
                copies.start(22 + h * 4 + j, part, part, heavy(h, -1))

    def ring_last(copies, buf):
        for h in range(2):
            for j in (2, 3):
                copies.arrived(6 + h * 8 + j * 2, buf.at[h, block(h, -j, -1)])
            for j in (0, 1):
                copies.arrived(6 + h * 8 + j * 2 + 1, buf.at[h, block(h, -j, 1)])
            for j in range(4):
                copies.arrived(22 + h * 4 + j, buf.at[h, block(h, -j, 2)])

    def gather_first(copies, buf):
        for d in (1, 3, 2):
            for h in range(2):
                copies.start(h * 3 + d - 1, buf.at[h, mine], buf.at[h, mine], light(h, d))
        gather_heavy(copies, buf, 0)

    def gather_heavy(copies, buf, j):
        for h in range(2):
            part = buf.at[h, block(h, -j, 0)]
            if j:
                copies.arrived(h * 3 + j - 1, part)
            for d in (1, 3, 2):
                copies.start(6 + h * 12 + j * 3 + d - 1, part, part, heavy(h, d))

    def gather_last(copies, buf):
        for j in range(4):
            for h in range(2):
                for d in (1, 3, 2):
                    copies.arrived(6 + h * 12 + j * 3 + d - 1, buf.at[h, block(h, -j, -d)])

    ring_first(wc, w_all)
    for e in range(2):
        target = lax.rem(c + e, 2)
        yc.start(e, y_sort.at[target], y_all.at[y, c], device(x, up, z, target), lands=c)
        yc.start(2 + e, y_sort.at[target], y_all.at[y, c], device(x, down, z, target), lands=2 + c)
    yc.start(4, y_sort.at[twin], y_all.at[y, c], device(x, y, z, twin))
    for k, (dx, dz) in enumerate(partners):
        xc.start(k, x_sort.at[at(x, dx) * 4 + at(z, dz)], x_mine.at[mine], device(at(x, dx), y, at(z, dz), c))
    y_all[y, c] = y_sort[c]
    x_mine[mine] = x_sort[mine]

    for j in (1, 3, 2):
        ring_heavy(wc, w_all, j)
    ring_forward(wc, w_all, 0)
    ring_forward(wc, w_all, 1)
    yc.arrived(0, y_all.at[down, 0])
    yc.start(5, y_all.at[down, 0], y_all.at[down, 0], device(x, up, z, c))
    yc.arrived(3, y_all.at[up, 1])
    yc.start(6, y_all.at[up, 1], y_all.at[up, 1], device(x, down, z, c))
    ring_forward(wc, w_all, 3)
    ring_forward(wc, w_all, 2)
    for k, (dx, dz) in enumerate(partners):
        xc.arrived(k, x_mine.at[at(x, -dx) * 4 + at(z, -dz)])
    yc.arrived(1, y_all.at[down, 1])
    yc.arrived(2, y_all.at[up, 0])

    def half(ref, k):
        return ref.at[k * 8 : k * 8 + 8]

    def x_half(s, e, k):
        return x_all.at[s, e, k * 8 : k * 8 + 8]

    for k in (0, 1):
        xyc.start(k, half(x_mine, k), x_half(y, c, k), device(x, up, z, c))
        xyc.start(3 - k, half(x_mine, 1 - k), x_half(y, c, 1 - k), device(x, down, z, c))
    xcc.start(0, x_mine, x_all.at[y, c], device(x, y, z, twin))
    x_all[y, c] = x_mine[...]

    ring_last(wc, w_all)
    yc.arrived(4, y_all.at[y, twin])
    yc.arrived(5, y_all.at[at(y, 2), 0])
    yc.arrived(6, y_all.at[at(y, 2), 1])

    part = jnp.zeros((192, 256), F32)
    for s in range(4):
        for h in range(2):
            part += jnp.dot(
                y_all[s, :, :, h * 512 : h * 512 + 512].reshape(192, 512),
                w_all[h, 4 * s : 4 * s + 4].reshape(512, 256),
                preferred_element_type=F32,
            )
    b_part[0] = part[:, :128]
    b_part[1] = part[:, 128:]
    pc.start(0, b_part.at[twin], b_other, device(x, y, z, twin))
    pc.arrived(0, b_other)
    for h in range(2):
        b_all[h, mine] = b_part[c, h * 96 : h * 96 + 96] + b_other[h * 96 : h * 96 + 96]
    gather_first(bc, b_all)

    xyc.arrived(0, x_half(down, c, 0))
    xyc.start(4, x_half(down, c, 0), x_half(down, c, 0), device(x, up, z, c))
    xyc.arrived(3, x_half(up, c, 1))
    xyc.start(5, x_half(up, c, 1), x_half(up, c, 1), device(x, down, z, c))
    for j in (1, 3, 2):
        gather_heavy(bc, b_all, j)
    xyc.arrived(1, x_half(down, c, 1))
    xcc.start(1, x_all.at[down, c], x_all.at[down, c], device(x, y, z, twin))
    xyc.arrived(2, x_half(up, c, 0))
    xcc.start(2, x_all.at[up, c], x_all.at[up, c], device(x, y, z, twin))
    xyc.arrived(4, x_half(at(y, 2), c, 0))
    xyc.arrived(5, x_half(at(y, 2), c, 1))
    xcc.start(3, x_all.at[at(y, 2), c], x_all.at[at(y, 2), c], device(x, y, z, twin))

    def arrange(s, e):
        piece = x_all[s, e].reshape(1536, 128)
        columns = pl.ds(pl.multiple_of(s * 128, 128), 128)
        rows = pl.ds(pl.multiple_of(e * 1536, 128), 1536)
        x_full[e, :, :, :, columns] = piece.reshape(4, 4, 96, 128)
        x_flip[columns, rows] = piece.T

    for s in (y, down, up, at(y, 2)):
        arrange(s, c)
    for k, s in enumerate((y, down, up, at(y, 2))):
        xcc.arrived(k, x_all.at[s, twin])
        arrange(s, twin)

    gather_last(bc, b_all)
    bb = jnp.zeros((1, 128), F32)
    for h in range(2):
        value = b_all[h].reshape(1536, 128)
        bb += jnp.sum(value * value, axis=0, keepdims=True)
        high, low = split(value)
        b_pair[h * 1536 : h * 1536 + 1536, :128] = high
        b_pair[h * 1536 : h * 1536 + 1536, 128:] = low
    wide = jnp.dot(x_flip[...], b_pair[...], preferred_element_type=F32)
    first = wide[:, :128] + wide[:, 128:]
    u0[...] = first.reshape(4, 128, 128)
    high, low = split(first * (1.0 / TOKENS))
    u_pair[:, :128] = high
    u_pair[:, 128:] = low

    def multiply(h, d):
        rows = x_full[0, at(x, d)] if h == 0 else x_full[1, :, at(z, d)]
        wide = jnp.dot(rows.reshape(384, 512), u_pair[...], preferred_element_type=F32)
        value = (wide[:, :128] + wide[:, 128:]).reshape(4, 96, 128)
        if h == 0:
            v_part[0, at(x, d)] = value
        else:
            v_part[1, :, at(z, d)] = value

    def pair(h, d, k):
        rows = slice(2 * k, 2 * k + 2)
        return v_part.at[0, at(x, d), rows] if h == 0 else v_part.at[1, rows, at(z, d)]

    def along(h, d):
        return heavy(1 - h, d)

    for h in range(2):
        multiply(h, 2)
        vc.start(30 + h * 2, pair(h, 2, 0), v_far.at[h, 0], along(h, 1))
        vc.start(31 + h * 2, pair(h, 2, 1), v_far.at[h, 1], along(h, -1))
    for h in range(2):
        multiply(h, 1)
        vc.start(34 + h * 2, pair(h, 1, 1), v_near.at[h, 0, 2:4], along(h, 1))
        multiply(h, -1)
        vc.start(35 + h * 2, pair(h, -1, 0), v_near.at[h, 1, 0:2], along(h, -1))
    for h in range(2):
        multiply(h, 0)
    for h in range(2):
        for k, d in ((0, 1), (1, -1)):
            vc.arrived(30 + h * 2 + k, v_far.at[h, k])
            v_merge[h, k] = pair(h, d, k)[...] + v_far[h, k]
            vc.start(38 + h * 2 + k, v_merge.at[h, k], v_near.at[h, k, 2 * k : 2 * k + 2], along(h, d))

    def hand_over(copies, buf, into):
        for p in range(4):
            place = at(x, p)
            target = device(place, y, x, owner)
            if p:
                copies.start(p, buf.at[place], into.at[slot], target, lands=slot)
            else:

                @pl.when(jnp.logical_not(stays))
                def _():
                    pltpu.make_async_remote_copy(
                        src_ref=buf.at[place], dst_ref=into.at[slot], send_sem=copies.send.at[0],
                        recv_sem=copies.recv.at[slot], device_id=target, device_id_type=MESH,
                    ).start()

                @pl.when(stays)
                def _():
                    pltpu.make_async_copy(buf.at[place], into.at[slot], copies.recv.at[slot]).start()

    hand_over(uc, u0, u_in)

    for h in range(2):
        vc.arrived(34 + h * 2, v_near.at[h, 0, 2:4])
        vc.arrived(35 + h * 2, v_near.at[h, 1, 0:2])
        vc.arrived(38 + h * 2, v_near.at[h, 0, 0:2])
        vc.arrived(39 + h * 2, v_near.at[h, 1, 2:4])
        own = v_part[0, x] if h == 0 else v_part[1, :, z]
        v_sum[h] = own + v_near[h, 0] + v_near[h, 1]
        for d in (1, 3, 2):
            lane = at(z, d) if h == 0 else at(x, d)
            vc.start(42 + h * 3 + d - 1, v_sum.at[h, lane], v_light.at[h, d - 1], light(1 - h, d))
    for h in range(2):
        for d in (1, 3, 2):
            vc.arrived(42 + h * 3 + d - 1, v_light.at[h, d - 1])
        lane = z if h == 0 else x
        v_all[h, mine] = v_sum[h, lane] + v_light[h, 0] + v_light[h, 1] + v_light[h, 2]
    gather_first(vc, v_all)
    for j in (1, 3, 2):
        gather_heavy(vc, v_all, j)
    gather_last(vc, v_all)

    bv = jnp.zeros((1, 128), F32)
    for h in range(2):
        bv += jnp.sum((b_all[h] * v_all[h]).reshape(1536, 128), axis=0, keepdims=True)
    alpha = bb / (bv + RIDGE * bb)
    norm = jnp.zeros((1, 128), F32)
    for h in range(2):
        value = b_all[h].reshape(1536, 128)
        residual = value - alpha * (v_all[h].reshape(1536, 128) + RIDGE * value)
        norm += jnp.sum(residual * residual, axis=0, keepdims=True)
        r_all[h] = residual
        high, low = split(residual)
        b_pair[h * 1536 : h * 1536 + 1536, :128] = high
        b_pair[h * 1536 : h * 1536 + 1536, 128:] = low
    beta = norm / bb
    wide = jnp.dot(x_flip[...], b_pair[...], preferred_element_type=F32)
    turned = wide[:, :128] + wide[:, 128:] + beta * u0[...].reshape(512, 128)
    ud[...] = turned.reshape(4, 128, 128)
    gamma[mine] = jnp.broadcast_to(jnp.sum(turned * turned, axis=0, keepdims=True), (8, 128))
    for k, (dx, dz) in enumerate(partners):
        gc.start(k, gamma.at[mine], gamma.at[mine], device(at(x, dx), y, at(z, dz), c))
    hand_over(dc, ud, d_in)
    dd = jnp.zeros((1, 128), F32)
    for h in range(2):
        turn = r_all[h] + beta * b_all[h].reshape(1536, 128)
        dd += jnp.sum(turn * turn, axis=0, keepdims=True)
    for k, (dx, dz) in enumerate(partners):
        gc.arrived(k, gamma.at[at(x, -dx) * 4 + at(z, -dz)])
    curve = jnp.sum(gamma[...], axis=0)[:1] * (1.0 / TOKENS) + RIDGE * dd
    step = norm / curve
    scalars[c] = jnp.concatenate(
        [jnp.broadcast_to(alpha * (1.0 / TOKENS), (8, 128)), jnp.broadcast_to(step * (1.0 / TOKENS), (8, 128))], axis=0
    )
    tc.start(0, scalars.at[c], scalars.at[c], device(x, y, z, twin))
    for k in range(4):
        uc.arrived(k, u_in.at[k])
        dc.arrived(k, d_in.at[k])
    tc.arrived(0, scalars.at[twin])
    for k in range(4):
        t, e = k // 2, k % 2
        out_ref[t * 128 : t * 128 + 128, e * 128 : e * 128 + 128] = (
            scalars[e, 0:1] * u_in[k] + scalars[e, 8:9] * d_in[k]
        )

    @pl.when(jnp.logical_not(stays))
    def _():
        pltpu.make_async_copy(u0.at[0], u0.at[0], u_s.at[0]).wait()
        pltpu.make_async_copy(ud.at[0], ud.at[0], d_s.at[0]).wait()

    for copies in (wc, yc, xc, bc, vc, xyc, xcc, pc, gc, tc, uc, dc):
        copies.finish()


def local(activations, targets, key_weight):
    dma = pltpu.SemaphoreType.DMA
    buffers = [
        ((16, 96, 128), BF16),
        ((2, 96, 1024), BF16),
        ((4, 2, 96, 1024), BF16),
        ((2, 16, 128, 256), BF16),
        ((16, 96, 128), BF16),
        ((4, 2, 16, 96, 128), BF16),
        ((2, 4, 4, 96, 512), BF16),
        ((512, TOKENS), BF16),
        ((2, 192, 128), F32),
        ((192, 128), F32),
        ((2, 16, 96, 128), F32),
        ((TOKENS, 256), BF16),
        ((4, 128, 128), F32),
        ((512, 256), BF16),
        ((4, 128, 128), F32),
        ((2, 4, 4, 96, 128), F32),
        ((2, 2, 2, 96, 128), F32),
        ((2, 2, 2, 96, 128), F32),
        ((2, 2, 4, 96, 128), F32),
        ((2, 4, 96, 128), F32),
        ((2, 3, 96, 128), F32),
        ((2, 16, 96, 128), F32),
        ((2, 1536, 128), F32),
        ((16, 8, 128), F32),
        ((2, 16, 128), F32),
        ((4, 128, 128), F32),
        ((4, 128, 128), F32),
    ]
    counts = (7, 30, 15, 6, 4, 1, 30, 48, 15, 1, 4, 4)
    return pl.pallas_call(
        kernel,
        out_shape=jax.ShapeDtypeStruct((256, 256), F32),
        in_specs=[pl.BlockSpec(memory_space=pl.ANY)] * 3,
        out_specs=pl.BlockSpec(memory_space=pltpu.VMEM),
        scratch_shapes=[pltpu.VMEM(*b) for b in buffers] + [dma((34,))] + [dma((n,)) for n in counts for _ in range(2)],
        compiler_params=pltpu.CompilerParams(collective_id=0, has_side_effects=True, vmem_limit_bytes=56 * 2**20),
    )(activations, targets, key_weight)


def solution(mesh):
    placed = (P("dp", "tensor"), P("dp", "tensor"), P("dp", "tensor"))
    return jax.shard_map(local, mesh=mesh, in_specs=placed, out_specs=P("dp", "tensor"), check_vma=False)
```

time: 99.4 us -> 87.8 us (0.88)
  Pallas kernels: 95.6 us -> 85.9 us
  local copies, waits for them, and re-layouts: 3.6 us -> 1.67 us
    pallas_call x1, Pallas kernels: 95.6 us -> 85.9 us  [local(): pl.pallas_call(kernel, out_shape=jax.ShapeDtypeStruct((256, 256), F32), i...]
    unnamed x7 -> x1, local copies, waits for them, and re-layouts: 3.6 us -> 1.67 us
where the time goes in v2:
time: 87.8 us; the launch traced here: 87.6 us
  Pallas kernels  85.9 us (98%)
  local copies, waits for them, and re-layouts  1.67 us (2%)
    pallas_call x1, Pallas kernels, local(): pl.pallas_call(kernel, out_shape=jax.ShapeDtypeStruct((256, 256), F32), i...  85.9 us

profile of v2, /device:TPU:1, one launch (start us, length us, event | category | flops | bytes accessed | tf_op | source)
XLA Modules:
  0.0 87.6 jit_solution(2041661798442238501)
XLA Ops:
  0.0 85.9 %shard_map.37 = f32[256,256]{1,0:T(8,128)} custom-call(bf16[96,2048]{1,0:T(8,128)(2,1)} %x_in.1, bf16[96,2048]{1,0:T(8,128)(2,1)} %y_in.1, bf16[256,256]{1,0:T(8,128)(2,1)} %w_in.1), custom_call_target="tpu_custom_call" | custom-call | tf_op jit(solution)/shard_map/pallas_call | solution.py:425
  85.9 1.7 %copy.5 = f32[256,256]{1,0:T(8,128)} copy(f32[256,256]{1,0:T(8,128)} %shard_map.37) | data formatting | bytes 524288

commit v3 on v2

v3 whole, which is shorter than its diff:
```python
import jax
import jax.numpy as jnp
from jax import lax
from jax.experimental import pallas as pl
from jax.experimental.pallas import tpu as pltpu
from jax.sharding import PartitionSpec as P

MESH = pl.DeviceIdType.MESH
TOKENS = 3072
RIDGE = 0.5
F32, BF16 = jnp.float32, jnp.bfloat16


def device(x, y, z, c):
    return (x * 8 + z * 2 + c, y)


def split(value):
    high = value.astype(BF16)
    return high, (value - high.astype(F32)).astype(BF16)


def encode(value):
    top = jnp.max(jnp.abs(value), axis=-2, keepdims=True)
    scale = jnp.maximum(top * 1.03125, 1e-30).astype(BF16)
    inverse = 8.0 / scale.astype(F32)
    p = jnp.abs(value) * inverse + 0.125
    p = p * p
    p = p * p
    p8 = p * p
    p = p8 * p8
    p = p * p * p8
    code = jnp.where(value < 0, -p, p).astype(BF16)
    return code, jnp.broadcast_to(scale, scale.shape[:-2] + (16, 128))


def decode(ref):
    code = ref[..., :96, :].astype(F32)
    scale = ref[..., 96:112, :].astype(F32)[..., :1, :] * 0.125
    p = jnp.exp2(jnp.log2(jnp.abs(code)) * (1.0 / 40.0))
    value = (p - 0.125) * scale
    return jnp.where(code < 0, -value, value)


def keep(ref, value):
    ref[..., :96, :], ref[..., 96:112, :] = encode(value)


class Copies:
    def __init__(self, send, recv):
        self.send, self.recv, self.started = send, recv, []

    def start(self, index, src, dst, target, lands=None):
        copy = pltpu.make_async_remote_copy(
            src_ref=src,
            dst_ref=dst,
            send_sem=self.send.at[index],
            recv_sem=self.recv.at[index if lands is None else lands],
            device_id=target,
            device_id_type=MESH,
        )
        copy.start()
        self.started.append(copy)
        return copy

    def arrived(self, index, dst):
        pltpu.make_async_copy(dst, dst, self.recv.at[index]).wait()

    def finish(self):
        for copy in self.started:
            copy.wait_send()


def kernel(
    x_in, y_in, w_in, out_ref,
    x_sort, y_sort, y_all, w_all, x_mine, x_all, x_full, x_flip,
    b_part, b_other, b_code, b_all, b_pair, u0, u_pair, ud,
    v_own, v_part, v_near, v_sum, v_send, v_light, v_code, v_all, r_all, gamma, scalars, u_in, d_in,
    l_s, y_s, y_r, w_s, w_r, x_s, x_r, xy_s, xy_r, xc_s, xc_r, p_s, p_r,
    b_s, b_r, v_s, v_r, g_s, g_r, t_s, t_r, u_s, u_r, d_s, d_r,
):
    i = lax.axis_index("dp")
    y = lax.axis_index("tensor")
    x, z, c = i // 8, lax.rem(i // 2, 4), lax.rem(i, 2)
    mine = x * 4 + z
    twin = 1 - c

    def at(a, d):
        return lax.rem(a + d + 4, 4)

    partners = [(dx, dz) for dx in range(4) for dz in range(4) if dx or dz]
    up, down = at(y, 1), at(y, -1)

    slot = lax.rem(z, 2) * 2 + c
    owner = z // 2
    stays = jnp.logical_and(x == z, owner == c)
    barrier = pltpu.get_barrier_semaphore()
    peers = [device(at(x, dx), y, at(z, dz), c) for dx, dz in partners]
    peers += [device(at(x, dx), y, at(z, dz), twin) for dx in range(4) for dz in range(4)]
    peers += [device(x, at(y, d), z, c) for d in (1, 2, 3)]
    peers += [device(x, place, z, twin) for place in (up, down)]
    for peer in peers:
        pl.semaphore_signal(barrier, inc=1, device_id=peer, device_id_type=MESH)

    loads = []
    for h in range(2):
        loads.append((w_in.at[h * 128 : h * 128 + 128, :], w_all.at[h, mine]))
    for e in range(2):
        for h in range(2):
            for q in range(4):
                columns = slice(q * 512 + e * 256 + h * 128, q * 512 + e * 256 + h * 128 + 128)
                loads.append((y_in.at[:, columns], y_sort.at[e, :, h * 512 + q * 128 : h * 512 + q * 128 + 128]))
    for k in range(16):
        loads.append((x_in.at[:, k * 128 : k * 128 + 128], x_sort.at[k]))
    loads = [pltpu.make_async_copy(src, dst, l_s.at[k]) for k, (src, dst) in enumerate(loads)]
    for load in loads:
        load.start()
    for load in loads[:2]:
        load.wait()
    pl.semaphore_wait(barrier, len(peers))

    wc, yc, xc, xyc, xcc = Copies(w_s, w_r), Copies(y_s, y_r), Copies(x_s, x_r), Copies(xy_s, xy_r), Copies(xc_s, xc_r)
    pc, bc, vc = Copies(p_s, p_r), Copies(b_s, b_r), Copies(v_s, v_r)
    gc, tc, uc, dc = Copies(g_s, g_r), Copies(t_s, t_r), Copies(u_s, u_r), Copies(d_s, d_r)

    def light(h, d):
        return device(at(x, d), y, z, c) if h == 0 else device(x, y, at(z, d), c)

    def heavy(h, d):
        return device(x, y, at(z, d), c) if h == 0 else device(at(x, d), y, z, c)

    def block(h, dl, dh):
        return at(x, dl) * 4 + at(z, dh) if h == 0 else at(x, dh) * 4 + at(z, dl)

    def gather_first(copies, buf):
        for d in (1, 3, 2):
            for h in range(2):
                copies.start(h * 3 + d - 1, buf.at[h, mine], buf.at[h, mine], light(h, d))
        gather_heavy(copies, buf, 0)

    def gather_heavy(copies, buf, j):
        for h in range(2):
            part = buf.at[h, block(h, -j, 0)]
            if j:
                copies.arrived(h * 3 + j - 1, part)
            for d in (1, 3, 2):
                copies.start(6 + h * 12 + j * 3 + d - 1, part, part, heavy(h, d))

    def gather_rest(copies, buf, use):
        for j in (1, 3, 2):
            gather_heavy(copies, buf, j)
        for h in range(2):
            for j in (0, 1, 3, 2):
                use(h, block(h, -j, 0))

    def gather_last(copies, buf, use):
        for j in (0, 1, 3, 2):
            for h in range(2):
                for d in (1, 3, 2):
                    place = block(h, -j, -d)
                    copies.arrived(6 + h * 12 + j * 3 + d - 1, buf.at[h, place])
                    use(h, place)

    gather_first(wc, w_all)

    def send_y(e, flip):
        target = lax.rem(c + e, 2)
        place = lax.rem(y + 1 + 2 * lax.rem(c + flip, 2), 4)
        return yc.start(flip * 2 + e, y_sort.at[target], y_all.at[y, c], device(x, place, z, target), lands=flip * 2 + c)

    for load in loads[2:18]:
        load.wait()
    first = [send_y(e, 0) for e in range(2)]
    for load in loads[18:]:
        load.wait()
    for k, (dx, dz) in enumerate(partners):
        xc.start(k, x_sort.at[at(x, dx) * 4 + at(z, dz)], x_mine.at[mine], device(at(x, dx), y, at(z, dz), c))
    y_all[y, c] = y_sort[c]
    x_mine[mine] = x_sort[mine]
    for copy in first:
        copy.wait_send()
        yc.started.remove(copy)
    for e in range(2):
        send_y(e, 1)
    yc.start(4, y_sort.at[twin], y_all.at[y, c], device(x, y, z, twin))

    for j in (1, 3, 2):
        gather_heavy(wc, w_all, j)
    yc.arrived(0, y_all.at[down, 0])
    yc.start(5, y_all.at[down, 0], y_all.at[down, 0], device(x, up, z, c))
    yc.arrived(1, y_all.at[up, 1])
    yc.start(6, y_all.at[up, 1], y_all.at[up, 1], device(x, down, z, c))
    for k, (dx, dz) in enumerate(partners):
        xc.arrived(k, x_mine.at[at(x, -dx) * 4 + at(z, -dz)])

    def x_half(s, e, k):
        return x_all.at[s, e, k * 8 : k * 8 + 8]

    def send_x(k, flip):
        place = up if k == flip else down
        xyc.start(flip * 2 + k, x_mine.at[k * 8 : k * 8 + 8], x_half(y, c, k), device(x, place, z, c))

    for k in range(2):
        send_x(k, 0)
    xcc.start(0, x_mine, x_all.at[y, c], device(x, y, z, twin))
    x_all[y, c] = x_mine[...]
    xyc.arrived(0, x_half(down, c, 0))
    xyc.start(4, x_half(down, c, 0), x_half(down, c, 0), device(x, up, z, c))
    xyc.arrived(1, x_half(up, c, 1))
    xyc.start(5, x_half(up, c, 1), x_half(up, c, 1), device(x, down, z, c))
    for k in range(2):
        send_x(k, 1)

    for h in range(2):
        for j in (0, 1, 3, 2):
            for d in (1, 3, 2):
                wc.arrived(6 + h * 12 + j * 3 + d - 1, w_all.at[h, block(h, -j, -d)])
    yc.arrived(2, y_all.at[up, 0])
    yc.arrived(3, y_all.at[down, 1])
    yc.arrived(4, y_all.at[y, twin])
    yc.arrived(5, y_all.at[at(y, 2), 0])
    yc.arrived(6, y_all.at[at(y, 2), 1])

    part = jnp.zeros((192, 256), F32)
    for s in range(4):
        for h in range(2):
            part += jnp.dot(
                y_all[s, :, :, h * 512 : h * 512 + 512].reshape(192, 512),
                w_all[h, 4 * s : 4 * s + 4].reshape(512, 256),
                preferred_element_type=F32,
            )
    b_part[0] = part[:, :128]
    b_part[1] = part[:, 128:]
    pc.start(0, b_part.at[twin], b_other, device(x, y, z, twin))
    pc.arrived(0, b_other)
    for h in range(2):
        keep(b_code.at[h, mine], b_part[c, h * 96 : h * 96 + 96] + b_other[h * 96 : h * 96 + 96])
    gather_first(bc, b_code)

    norms = []

    def use_b(h, place):
        value = decode(b_code.at[h, place])
        b_all[h, place] = value
        norms.append(jnp.sum(value * value, axis=0, keepdims=True))
        high, low = split(value)
        b_pair[h, place, :, :128] = high
        b_pair[h, place, :, 128:] = low

    gather_rest(bc, b_code, use_b)
    xyc.arrived(2, x_half(up, c, 0))
    xcc.start(3, x_all.at[up, c], x_all.at[up, c], device(x, y, z, twin))
    xyc.arrived(3, x_half(down, c, 1))
    xcc.start(1, x_all.at[down, c], x_all.at[down, c], device(x, y, z, twin))
    xyc.arrived(4, x_half(at(y, 2), c, 0))
    xyc.arrived(5, x_half(at(y, 2), c, 1))
    xcc.start(2, x_all.at[at(y, 2), c], x_all.at[at(y, 2), c], device(x, y, z, twin))

    def arrange(s, e):
        piece = x_all[s, e].reshape(1536, 128)
        columns = pl.ds(pl.multiple_of(s * 128, 128), 128)
        rows = pl.ds(pl.multiple_of(e * 1536, 128), 1536)
        x_full[e, :, :, :, columns] = piece.reshape(4, 4, 96, 128)
        x_flip[columns, rows] = piece.T

    for d in (0, 1, 3, 2):
        arrange(at(y, -d), c)
    for d in (0, 1, 3, 2):
        xcc.arrived(d, x_all.at[at(y, -d), twin])
        arrange(at(y, -d), twin)

    gather_last(bc, b_code, use_b)
    bb = sum(norms)
    wide = jnp.dot(x_flip[...], b_pair[...].reshape(TOKENS, 256), preferred_element_type=F32)
    first = wide[:, :128] + wide[:, 128:]
    u0[...] = first.reshape(4, 128, 128)
    high, low = split(first * (1.0 / TOKENS))
    u_pair[:, :128] = high
    u_pair[:, 128:] = low

    def multiply(h, d):
        rows = x_full[0, at(x, d)] if h == 0 else x_full[1, :, at(z, d)]
        wide = jnp.dot(rows.reshape(384, 512), u_pair[...], preferred_element_type=F32)
        value = (wide[:, :128] + wide[:, 128:]).reshape(4, 96, 128)
        if d == 0:
            v_own[h] = value
        else:
            keep(v_part.at[h, d - 1], value)
            vc.start(30 + h * 3 + d - 1, v_part.at[h, d - 1], v_near.at[h, d - 1], heavy(1 - h, d))

    for d in (2, 1, 3, 0):
        for h in range(2):
            multiply(h, d)

    def hand_over(copies, buf, into):
        for p in range(4):
            place = at(x, p)
            target = device(place, y, x, owner)
            if p:
                copies.start(p, buf.at[place], into.at[slot], target, lands=slot)
            else:

                @pl.when(jnp.logical_not(stays))
                def _():
                    pltpu.make_async_remote_copy(
                        src_ref=buf.at[place], dst_ref=into.at[slot], send_sem=copies.send.at[0],
                        recv_sem=copies.recv.at[slot], device_id=target, device_id_type=MESH,
                    ).start()

                @pl.when(stays)
                def _():
                    pltpu.make_async_copy(buf.at[place], into.at[slot], copies.recv.at[slot]).start()

    hand_over(uc, u0, u_in)

    for h in range(2):
        total = v_own[h]
        for d in (1, 3, 2):
            vc.arrived(30 + h * 3 + d - 1, v_near.at[h, d - 1])
            total += decode(v_near.at[h, d - 1])
        v_sum[h] = total
        keep(v_send.at[h], total)
        for d in (1, 3, 2):
            lane = at(z, d) if h == 0 else at(x, d)
            vc.start(36 + h * 3 + d - 1, v_send.at[h, lane], v_light.at[h, d - 1], light(1 - h, d))
    for h in range(2):
        total = v_sum[h, z if h == 0 else x]
        for d in (1, 3, 2):
            vc.arrived(36 + h * 3 + d - 1, v_light.at[h, d - 1])
            total += decode(v_light.at[h, d - 1])
        keep(v_code.at[h, mine], total)
    gather_first(vc, v_code)

    dots = []

    def use_v(h, place):
        value = decode(v_code.at[h, place])
        v_all[h, place] = value
        dots.append(jnp.sum(value * b_all[h, place], axis=0, keepdims=True))

    gather_rest(vc, v_code, use_v)
    gather_last(vc, v_code, use_v)

    bv = sum(dots)
    alpha = bb / (bv + RIDGE * bb)
    norm = jnp.zeros((1, 128), F32)
    for h in range(2):
        value = b_all[h].reshape(1536, 128)
        residual = value - alpha * (v_all[h].reshape(1536, 128) + RIDGE * value)
        norm += jnp.sum(residual * residual, axis=0, keepdims=True)
        r_all[h] = residual
        high, low = split(residual)
        b_pair[h, :, :, :128] = high.reshape(16, 96, 128)
        b_pair[h, :, :, 128:] = low.reshape(16, 96, 128)
    beta = norm / bb
    wide = jnp.dot(x_flip[...], b_pair[...].reshape(TOKENS, 256), preferred_element_type=F32)
    turned = wide[:, :128] + wide[:, 128:] + beta * u0[...].reshape(512, 128)
    ud[...] = turned.reshape(4, 128, 128)
    gamma[c, mine] = jnp.broadcast_to(jnp.sum(turned * turned, axis=0, keepdims=True), (8, 128))
    spread = [(dx, dz, e) for dx in (2, 1, 3, 0) for dz in (2, 1, 3, 0) for e in (0, 1) if dx or dz or e]
    for k, (dx, dz, e) in enumerate(spread):
        gc.start(k, gamma.at[c, mine], gamma.at[c, mine], device(at(x, dx), y, at(z, dz), lax.rem(c + e, 2)))
    hand_over(dc, ud, d_in)
    dd = jnp.zeros((1, 128), F32)
    for h in range(2):
        turn = r_all[h] + beta * b_all[h].reshape(1536, 128)
        dd += jnp.sum(turn * turn, axis=0, keepdims=True)
    scalars[c, 0] = jnp.broadcast_to(alpha * (1.0 / TOKENS), (8, 128))
    scalars[c, 1] = jnp.broadcast_to(norm * (1.0 / TOKENS), (8, 128))
    scalars[c, 2] = jnp.broadcast_to(dd * RIDGE, (8, 128))
    tc.start(0, scalars.at[c], scalars.at[c], device(x, y, z, twin))
    tc.arrived(0, scalars.at[twin])
    for k, (dx, dz, e) in enumerate(spread):
        gc.arrived(k, gamma.at[lax.rem(c + e, 2), at(x, -dx) * 4 + at(z, -dz)])
    steps = []
    for e in range(2):
        curve = jnp.sum(gamma[e], axis=0)[:1] * (1.0 / TOKENS) + scalars[e, 2, :1]
        steps.append(scalars[e, 1, :1] / curve)
    for k in range(4):
        uc.arrived(k, u_in.at[k])
        dc.arrived(k, d_in.at[k])
    for k in range(4):
        t, e = k // 2, k % 2
        out_ref[t * 128 : t * 128 + 128, e * 128 : e * 128 + 128] = (
            scalars[e, 0, :1] * u_in[k] + steps[e] * d_in[k]
        )

    @pl.when(jnp.logical_not(stays))
    def _():
        pltpu.make_async_copy(u0.at[0], u0.at[0], u_s.at[0]).wait()
        pltpu.make_async_copy(ud.at[0], ud.at[0], d_s.at[0]).wait()

    for copies in (wc, yc, xc, bc, vc, xyc, xcc, pc, gc, tc, uc, dc):
        copies.finish()


def local(activations, targets, key_weight):
    dma = pltpu.SemaphoreType.DMA
    buffers = [
        ((16, 96, 128), BF16),
        ((2, 96, 1024), BF16),
        ((4, 2, 96, 1024), BF16),
        ((2, 16, 128, 256), BF16),
        ((16, 96, 128), BF16),
        ((4, 2, 16, 96, 128), BF16),
        ((2, 4, 4, 96, 512), BF16),
        ((512, TOKENS), BF16),
        ((2, 192, 128), F32),
        ((192, 128), F32),
        ((2, 16, 112, 128), BF16),
        ((2, 16, 96, 128), F32),
        ((2, 16, 96, 256), BF16),
        ((4, 128, 128), F32),
        ((512, 256), BF16),
        ((4, 128, 128), F32),
        ((2, 4, 96, 128), F32),
        ((2, 3, 4, 112, 128), BF16),
        ((2, 3, 4, 112, 128), BF16),
        ((2, 4, 96, 128), F32),
        ((2, 4, 112, 128), BF16),
        ((2, 3, 112, 128), BF16),
        ((2, 16, 112, 128), BF16),
        ((2, 16, 96, 128), F32),
        ((2, 1536, 128), F32),
        ((2, 16, 8, 128), F32),
        ((2, 3, 8, 128), F32),
        ((4, 128, 128), F32),
        ((4, 128, 128), F32),
    ]
    counts = (7, 30, 15, 6, 4, 1, 30, 42, 31, 1, 4, 4)
    return pl.pallas_call(
        kernel,
        out_shape=jax.ShapeDtypeStruct((256, 256), F32),
        in_specs=[pl.BlockSpec(memory_space=pl.ANY)] * 3,
        out_specs=pl.BlockSpec(memory_space=pltpu.VMEM),
        scratch_shapes=[pltpu.VMEM(*b) for b in buffers] + [dma((34,))] + [dma((n,)) for n in counts for _ in range(2)],
        compiler_params=pltpu.CompilerParams(collective_id=0, has_side_effects=True, vmem_limit_bytes=56 * 2**20),
    )(activations, targets, key_weight)


def solution(mesh):
    placed = (P("dp", "tensor"), P("dp", "tensor"), P("dp", "tensor"))
    return jax.shard_map(local, mesh=mesh, in_specs=placed, out_specs=P("dp", "tensor"), check_vma=False)
```

time: 87.8 us -> 80.6 us (0.918)
  Pallas kernels: 85.9 us -> 78.8 us
    pallas_call x1, Pallas kernels: 85.9 us -> 78.8 us  [local(): pl.pallas_call(kernel, out_shape=jax.ShapeDtypeStruct((256, 256), F32), i...]
where the time goes in v3:
time: 80.6 us; the launch traced here: 80.4 us
  Pallas kernels  78.8 us (98%)
  local copies, waits for them, and re-layouts  1.67 us (2%)
    pallas_call x1, Pallas kernels, local(): pl.pallas_call(kernel, out_shape=jax.ShapeDtypeStruct((256, 256), F32), i...  78.8 us
    unnamed x1, local copies, waits for them, and re-layouts  1.67 us

profile of v3, /device:TPU:1, one launch (start us, length us, event | category | flops | bytes accessed | tf_op | source)
XLA Modules:
  0.0 80.4 jit_solution(1455349607695870636)
XLA Ops:
  0.0 78.8 %shard_map.37 = f32[256,256]{1,0:T(8,128)} custom-call(bf16[96,2048]{1,0:T(8,128)(2,1)} %x_in.1, bf16[96,2048]{1,0:T(8,128)(2,1)} %y_in.1, bf16[256,256]{1,0:T(8,128)(2,1)} %w_in.1), custom_call_target="tpu_custom_call" | custom-call | tf_op jit(solution)/shard_map/pallas_call | solution.py:431
  78.8 1.7 %copy.5 = f32[256,256]{1,0:T(8,128)} copy(f32[256,256]{1,0:T(8,128)} %shard_map.37) | data formatting | bytes 524288

commit v4 on v3

--- a/solution.py
+++ b/solution.py
@@ -35,15 +35,17 @@
 
 
 def decode(ref):
-    code = ref[..., :96, :].astype(F32)
-    scale = ref[..., 96:112, :].astype(F32)[..., :1, :] * 0.125
+    rows = ref.shape[-2] - 16
+    code = ref[..., :rows, :].astype(F32)
+    scale = ref[..., rows:, :].astype(F32)[..., :1, :] * 0.125
     p = jnp.exp2(jnp.log2(jnp.abs(code)) * (1.0 / 40.0))
     value = (p - 0.125) * scale
     return jnp.where(code < 0, -value, value)
 
 
 def keep(ref, value):
-    ref[..., :96, :], ref[..., 96:112, :] = encode(value)
+    rows = value.shape[-2]
+    ref[..., :rows, :], ref[..., rows:, :] = encode(value)
 
 
 class Copies:
@@ -61,7 +63,6 @@
         )
         copy.start()
         self.started.append(copy)
-        return copy
 
     def arrived(self, index, dst):
         pltpu.make_async_copy(dst, dst, self.recv.at[index]).wait()
@@ -74,8 +75,8 @@
 def kernel(
     x_in, y_in, w_in, out_ref,
     x_sort, y_sort, y_all, w_all, x_mine, x_all, x_full, x_flip,
-    b_part, b_other, b_code, b_all, b_pair, u0, u_pair, ud,
-    v_own, v_part, v_near, v_sum, v_send, v_light, v_code, v_all, r_all, gamma, scalars, u_in, d_in,
+    b_part, b_other, b_code, b_all, b_pair, u0, u_pair, u_code, d_code,
+    v_own, v_part, v_near, v_send, v_line, v_code, v_all, r_all, gamma, scalars, u_in, d_in,
     l_s, y_s, y_r, w_s, w_r, x_s, x_r, xy_s, xy_r, xc_s, xc_r, p_s, p_r,
     b_s, b_r, v_s, v_r, g_s, g_r, t_s, t_r, u_s, u_r, d_s, d_r,
 ):
@@ -115,7 +116,7 @@
     loads = [pltpu.make_async_copy(src, dst, l_s.at[k]) for k, (src, dst) in enumerate(loads)]
     for load in loads:
         load.start()
-    for load in loads[:2]:
+    for load in loads:
         load.wait()
     pl.semaphore_wait(barrier, len(peers))
 
@@ -161,31 +162,37 @@
                     copies.arrived(6 + h * 12 + j * 3 + d - 1, buf.at[h, place])
                     use(h, place)
 
-    gather_first(wc, w_all)
-
-    def send_y(e, flip):
-        target = lax.rem(c + e, 2)
-        place = lax.rem(y + 1 + 2 * lax.rem(c + flip, 2), 4)
-        return yc.start(flip * 2 + e, y_sort.at[target], y_all.at[y, c], device(x, place, z, target), lands=flip * 2 + c)
-
-    for load in loads[2:18]:
-        load.wait()
-    first = [send_y(e, 0) for e in range(2)]
-    for load in loads[18:]:
-        load.wait()
+    def ring_heavy(j):
+        for h in range(2):
+            part = w_all.at[h, block(h, -j, 0)]
+            if j:
+                wc.arrived(h * 3 + j - 1, part)
+            wc.start(6 + h * 8 + j * 2, part, part, heavy(h, 1))
+            wc.start(6 + h * 8 + j * 2 + 1, part, part, heavy(h, -1))
+
+    def ring_forward(j):
+        for h in range(2):
+            k, d = (0, 1) if j in (0, 1) else (1, -1)
+            part = w_all.at[h, block(h, -j, -d)]
+            wc.arrived(6 + h * 8 + j * 2 + k, part)
+            wc.start(22 + h * 4 + j, part, part, heavy(h, d))
+
     for k, (dx, dz) in enumerate(partners):
         xc.start(k, x_sort.at[at(x, dx) * 4 + at(z, dz)], x_mine.at[mine], device(at(x, dx), y, at(z, dz), c))
+
+    for flip in range(2):
+        for e in range(2):
+            target = lax.rem(c + e, 2)
+            place = lax.rem(y + 1 + 2 * lax.rem(c + flip, 2), 4)
+            yc.start(flip * 2 + e, y_sort.at[target], y_all.at[y, c], device(x, place, z, target), lands=flip * 2 + c)
+    for d in (1, 3, 2):
+        for h in range(2):
+            wc.start(h * 3 + d - 1, w_all.at[h, mine], w_all.at[h, mine], light(h, d))
+    ring_heavy(0)
+    yc.start(4, y_sort.at[twin], y_all.at[y, c], device(x, y, z, twin))
     y_all[y, c] = y_sort[c]
     x_mine[mine] = x_sort[mine]
-    for copy in first:
-        copy.wait_send()
-        yc.started.remove(copy)
-    for e in range(2):
-        send_y(e, 1)
-    yc.start(4, y_sort.at[twin], y_all.at[y, c], device(x, y, z, twin))
-
-    for j in (1, 3, 2):
-        gather_heavy(wc, w_all, j)
+
     yc.arrived(0, y_all.at[down, 0])
     yc.start(5, y_all.at[down, 0], y_all.at[down, 0], device(x, up, z, c))
     yc.arrived(1, y_all.at[up, 1])
@@ -196,25 +203,27 @@
     def x_half(s, e, k):
         return x_all.at[s, e, k * 8 : k * 8 + 8]
 
-    def send_x(k, flip):
-        place = up if k == flip else down
-        xyc.start(flip * 2 + k, x_mine.at[k * 8 : k * 8 + 8], x_half(y, c, k), device(x, place, z, c))
-
-    for k in range(2):
-        send_x(k, 0)
+    for flip in range(2):
+        for k in range(2):
+            place = up if k == flip else down
+            xyc.start(flip * 2 + k, x_mine.at[k * 8 : k * 8 + 8], x_half(y, c, k), device(x, place, z, c))
     xcc.start(0, x_mine, x_all.at[y, c], device(x, y, z, twin))
+    for j in (1, 3, 2):
+        ring_heavy(j)
     x_all[y, c] = x_mine[...]
+    for j in (0, 1, 3, 2):
+        ring_forward(j)
     xyc.arrived(0, x_half(down, c, 0))
     xyc.start(4, x_half(down, c, 0), x_half(down, c, 0), device(x, up, z, c))
     xyc.arrived(1, x_half(up, c, 1))
     xyc.start(5, x_half(up, c, 1), x_half(up, c, 1), device(x, down, z, c))
-    for k in range(2):
-        send_x(k, 1)
-
     for h in range(2):
-        for j in (0, 1, 3, 2):
-            for d in (1, 3, 2):
-                wc.arrived(6 + h * 12 + j * 3 + d - 1, w_all.at[h, block(h, -j, -d)])
+        for j in (2, 3):
+            wc.arrived(6 + h * 8 + j * 2, w_all.at[h, block(h, -j, -1)])
+        for j in (0, 1):
+            wc.arrived(6 + h * 8 + j * 2 + 1, w_all.at[h, block(h, -j, 1)])
+        for j in range(4):
+            wc.arrived(22 + h * 4 + j, w_all.at[h, block(h, -j, 2)])
     yc.arrived(2, y_all.at[up, 0])
     yc.arrived(3, y_all.at[down, 1])
     yc.arrived(4, y_all.at[y, twin])
@@ -278,20 +287,6 @@
     u_pair[:, :128] = high
     u_pair[:, 128:] = low
 
-    def multiply(h, d):
-        rows = x_full[0, at(x, d)] if h == 0 else x_full[1, :, at(z, d)]
-        wide = jnp.dot(rows.reshape(384, 512), u_pair[...], preferred_element_type=F32)
-        value = (wide[:, :128] + wide[:, 128:]).reshape(4, 96, 128)
-        if d == 0:
-            v_own[h] = value
-        else:
-            keep(v_part.at[h, d - 1], value)
-            vc.start(30 + h * 3 + d - 1, v_part.at[h, d - 1], v_near.at[h, d - 1], heavy(1 - h, d))
-
-    for d in (2, 1, 3, 0):
-        for h in range(2):
-            multiply(h, d)
-
     def hand_over(copies, buf, into):
         for p in range(4):
             place = at(x, p)
@@ -311,35 +306,68 @@
                 def _():
                     pltpu.make_async_copy(buf.at[place], into.at[slot], copies.recv.at[slot]).start()
 
-    hand_over(uc, u0, u_in)
-
-    for h in range(2):
-        total = v_own[h]
-        for d in (1, 3, 2):
-            vc.arrived(30 + h * 3 + d - 1, v_near.at[h, d - 1])
-            total += decode(v_near.at[h, d - 1])
-        v_sum[h] = total
-        keep(v_send.at[h], total)
-        for d in (1, 3, 2):
-            lane = at(z, d) if h == 0 else at(x, d)
-            vc.start(36 + h * 3 + d - 1, v_send.at[h, lane], v_light.at[h, d - 1], light(1 - h, d))
-    for h in range(2):
-        total = v_sum[h, z if h == 0 else x]
-        for d in (1, 3, 2):
-            vc.arrived(36 + h * 3 + d - 1, v_light.at[h, d - 1])
-            total += decode(v_light.at[h, d - 1])
-        keep(v_code.at[h, mine], total)
-    gather_first(vc, v_code)
+    def along(h, d):
+        return heavy(1 - h, d)
+
+    def multiply(h, s, d):
+        lanes = slice(2 * s, 2 * s + 2)
+        rows = x_full[0, at(x, d), lanes] if h == 0 else x_full[1, lanes, at(z, d)]
+        wide = jnp.dot(rows.reshape(192, 512), u_pair[...], preferred_element_type=F32)
+        value = (wide[:, :128] + wide[:, 128:]).reshape(2, 96, 128)
+        if d == 0:
+            v_own[h, s] = value
+        else:
+            keep(v_part.at[h, s, d - 1], value)
+            vc.start(h * 6 + s * 3 + d - 1, v_part.at[h, s, d - 1], v_near.at[h, s, d - 1], along(h, d))
+
+    for s in range(2):
+        for d in (2, 1, 3):
+            for h in range(2):
+                multiply(h, s, d)
+    keep(u_code, u0[...])
+    hand_over(uc, u_code, u_in)
+    for s in range(2):
+        for h in range(2):
+            multiply(h, s, 0)
+    for s in range(2):
+        for h in range(2):
+            total = v_own[h, s]
+            for d in (1, 3, 2):
+                vc.arrived(h * 6 + s * 3 + d - 1, v_near.at[h, s, d - 1])
+                total += decode(v_near.at[h, s, d - 1])
+            keep(v_send.at[h, s], total)
+            for d in (1, 3, 2):
+                vc.start(12 + h * 6 + s * 3 + d - 1, v_send.at[h, s], v_line.at[h, s, d - 1], heavy(h, d))
 
     dots = []
 
-    def use_v(h, place):
-        value = decode(v_code.at[h, place])
-        v_all[h, place] = value
-        dots.append(jnp.sum(value * b_all[h, place], axis=0, keepdims=True))
-
-    gather_rest(vc, v_code, use_v)
-    gather_last(vc, v_code, use_v)
+    def use_v(h, s, d):
+        along_place = at(x if h == 0 else z, -d)
+        value = decode(v_code.at[h, along_place, 2 * s : 2 * s + 2])
+        for k in range(2):
+            lane = 2 * s + k
+            place = along_place * 4 + lane if h == 0 else lane * 4 + along_place
+            v_all[h, place] = value[k]
+            dots.append(jnp.sum(value[k] * b_all[h, place], axis=0, keepdims=True))
+
+    for s in range(2):
+        for h in range(2):
+            total = decode(v_send.at[h, s])
+            for d in (1, 3, 2):
+                vc.arrived(12 + h * 6 + s * 3 + d - 1, v_line.at[h, s, d - 1])
+                total += decode(v_line.at[h, s, d - 1])
+            mine_here = v_code.at[h, x if h == 0 else z, 2 * s : 2 * s + 2]
+            keep(mine_here, total)
+            for d in (1, 3, 2):
+                vc.start(24 + h * 6 + s * 3 + d - 1, mine_here, mine_here, along(h, d))
+            use_v(h, s, 0)
+    for s in range(2):
+        for h in range(2):
+            for d in (1, 3, 2):
+                vc.arrived(
+                    24 + h * 6 + s * 3 + d - 1, v_code.at[h, at(x if h == 0 else z, -d), 2 * s : 2 * s + 2]
+                )
+                use_v(h, s, d)
 
     bv = sum(dots)
     alpha = bb / (bv + RIDGE * bb)
@@ -355,12 +383,12 @@
     beta = norm / bb
     wide = jnp.dot(x_flip[...], b_pair[...].reshape(TOKENS, 256), preferred_element_type=F32)
     turned = wide[:, :128] + wide[:, 128:] + beta * u0[...].reshape(512, 128)
-    ud[...] = turned.reshape(4, 128, 128)
+    keep(d_code, turned.reshape(4, 128, 128))
     gamma[c, mine] = jnp.broadcast_to(jnp.sum(turned * turned, axis=0, keepdims=True), (8, 128))
     spread = [(dx, dz, e) for dx in (2, 1, 3, 0) for dz in (2, 1, 3, 0) for e in (0, 1) if dx or dz or e]
     for k, (dx, dz, e) in enumerate(spread):
         gc.start(k, gamma.at[c, mine], gamma.at[c, mine], device(at(x, dx), y, at(z, dz), lax.rem(c + e, 2)))
-    hand_over(dc, ud, d_in)
+    hand_over(dc, d_code, d_in)
     dd = jnp.zeros((1, 128), F32)
     for h in range(2):
         turn = r_all[h] + beta * b_all[h].reshape(1536, 128)
@@ -382,13 +410,13 @@
     for k in range(4):
         t, e = k // 2, k % 2
         out_ref[t * 128 : t * 128 + 128, e * 128 : e * 128 + 128] = (
-            scalars[e, 0, :1] * u_in[k] + steps[e] * d_in[k]
+            scalars[e, 0, :1] * decode(u_in.at[k]) + steps[e] * decode(d_in.at[k])
         )
 
     @pl.when(jnp.logical_not(stays))
     def _():
-        pltpu.make_async_copy(u0.at[0], u0.at[0], u_s.at[0]).wait()
-        pltpu.make_async_copy(ud.at[0], ud.at[0], d_s.at[0]).wait()
+        pltpu.make_async_copy(u_code.at[0], u_code.at[0], u_s.at[0]).wait()
+        pltpu.make_async_copy(d_code.at[0], d_code.at[0], d_s.at[0]).wait()
 
     for copies in (wc, yc, xc, bc, vc, xyc, xcc, pc, gc, tc, uc, dc):
         copies.finish()
@@ -412,22 +440,22 @@
         ((2, 16, 96, 256), BF16),
         ((4, 128, 128), F32),
         ((512, 256), BF16),
-        ((4, 128, 128), F32),
-        ((2, 4, 96, 128), F32),
-        ((2, 3, 4, 112, 128), BF16),
-        ((2, 3, 4, 112, 128), BF16),
-        ((2, 4, 96, 128), F32),
-        ((2, 4, 112, 128), BF16),
-        ((2, 3, 112, 128), BF16),
-        ((2, 16, 112, 128), BF16),
+        ((4, 144, 128), BF16),
+        ((4, 144, 128), BF16),
+        ((2, 2, 2, 96, 128), F32),
+        ((2, 2, 3, 2, 112, 128), BF16),
+        ((2, 2, 3, 2, 112, 128), BF16),
+        ((2, 2, 2, 112, 128), BF16),
+        ((2, 2, 3, 2, 112, 128), BF16),
+        ((2, 4, 4, 112, 128), BF16),
         ((2, 16, 96, 128), F32),
         ((2, 1536, 128), F32),
         ((2, 16, 8, 128), F32),
         ((2, 3, 8, 128), F32),
-        ((4, 128, 128), F32),
-        ((4, 128, 128), F32),
+        ((4, 144, 128), BF16),
+        ((4, 144, 128), BF16),
     ]
-    counts = (7, 30, 15, 6, 4, 1, 30, 42, 31, 1, 4, 4)
+    counts = (7, 30, 15, 6, 4, 1, 30, 36, 31, 1, 4, 4)
     return pl.pallas_call(
         kernel,
         out_shape=jax.ShapeDtypeStruct((256, 256), F32),

time: 80.6 us -> 76.1 us (0.944)
  Pallas kernels: 78.8 us -> 74.2 us
    pallas_call x1, Pallas kernels: 78.8 us -> 74.2 us  [local(): pl.pallas_call(kernel, out_shape=jax.ShapeDtypeStruct((256, 256), F32), i...]
where the time goes in v4:
time: 76.1 us; the launch traced here: 75.9 us
  Pallas kernels  74.2 us (98%)
  local copies, waits for them, and re-layouts  1.67 us (2%)
    pallas_call x1, Pallas kernels, local(): pl.pallas_call(kernel, out_shape=jax.ShapeDtypeStruct((256, 256), F32), i...  74.2 us
    unnamed x1, local copies, waits for them, and re-layouts  1.67 us

profile of v4, /device:TPU:1, one launch (start us, length us, event | category | flops | bytes accessed | tf_op | source)
XLA Modules:
  0.0 75.9 jit_solution(15364087280056163450)
XLA Ops:
  0.0 74.2 %shard_map.37 = f32[256,256]{1,0:T(8,128)} custom-call(bf16[96,2048]{1,0:T(8,128)(2,1)} %x_in.1, bf16[96,2048]{1,0:T(8,128)(2,1)} %y_in.1, bf16[256,256]{1,0:T(8,128)(2,1)} %w_in.1), custom_call_target="tpu_custom_call" | custom-call | tf_op jit(solution)/shard_map/pallas_call | solution.py:459
  74.2 1.7 %copy.5 = f32[256,256]{1,0:T(8,128)} copy(f32[256,256]{1,0:T(8,128)} %shard_map.37) | data formatting | bytes 524288

commit v5 on v4

--- a/solution.py
+++ b/solution.py
@@ -78,7 +78,7 @@
     b_part, b_other, b_code, b_all, b_pair, u0, u_pair, u_code, d_code,
     v_own, v_part, v_near, v_send, v_line, v_code, v_all, r_all, gamma, scalars, u_in, d_in,
     l_s, y_s, y_r, w_s, w_r, x_s, x_r, xy_s, xy_r, xc_s, xc_r, p_s, p_r,
-    b_s, b_r, v_s, v_r, g_s, g_r, t_s, t_r, u_s, u_r, d_s, d_r,
+    b_s, b_r, v_s, v_r, g_s, g_r, t_s, t_r, u_s, u_r, d_s, d_r, line_sem, twin_sem,
 ):
     i = lax.axis_index("dp")
     y = lax.axis_index("tensor")
@@ -96,10 +96,9 @@
     owner = z // 2
     stays = jnp.logical_and(x == z, owner == c)
     barrier = pltpu.get_barrier_semaphore()
-    peers = [device(at(x, dx), y, at(z, dz), c) for dx, dz in partners]
-    peers += [device(at(x, dx), y, at(z, dz), twin) for dx in range(4) for dz in range(4)]
-    peers += [device(x, at(y, d), z, c) for d in (1, 2, 3)]
-    peers += [device(x, place, z, twin) for place in (up, down)]
+    peers = [device(at(x, d), y, z, c) for d in (1, 3, 2)] + [device(x, y, at(z, d), c) for d in (1, 3, 2)]
+    peers += [device(x, place, z, e) for place in (up, down) for e in (c, twin)]
+    peers += [device(x, y, z, twin)]
     for peer in peers:
         pl.semaphore_signal(barrier, inc=1, device_id=peer, device_id_type=MESH)
 
@@ -119,6 +118,8 @@
     for load in loads:
         load.wait()
     pl.semaphore_wait(barrier, len(peers))
+    for d in (1, 3, 2):
+        pl.semaphore_signal(line_sem, inc=1, device_id=device(at(x, d), y, z, c), device_id_type=MESH)
 
     wc, yc, xc, xyc, xcc = Copies(w_s, w_r), Copies(y_s, y_r), Copies(x_s, x_r), Copies(xy_s, xy_r), Copies(xc_s, xc_r)
     pc, bc, vc = Copies(p_s, p_r), Copies(b_s, b_r), Copies(v_s, v_r)
@@ -177,9 +178,6 @@
             wc.arrived(6 + h * 8 + j * 2 + k, part)
             wc.start(22 + h * 4 + j, part, part, heavy(h, d))
 
-    for k, (dx, dz) in enumerate(partners):
-        xc.start(k, x_sort.at[at(x, dx) * 4 + at(z, dz)], x_mine.at[mine], device(at(x, dx), y, at(z, dz), c))
-
     for flip in range(2):
         for e in range(2):
             target = lax.rem(c + e, 2)
@@ -189,6 +187,10 @@
         for h in range(2):
             wc.start(h * 3 + d - 1, w_all.at[h, mine], w_all.at[h, mine], light(h, d))
     ring_heavy(0)
+    pl.semaphore_wait(line_sem, 3)
+    for k, (dx, dz) in enumerate(partners):
+        xc.start(k, x_sort.at[at(x, dx) * 4 + at(z, dz)], x_mine.at[mine], device(at(x, dx), y, at(z, dz), c))
+    pl.semaphore_signal(twin_sem, inc=1, device_id=device(x, y, z, twin), device_id_type=MESH)
     yc.start(4, y_sort.at[twin], y_all.at[y, c], device(x, y, z, twin))
     y_all[y, c] = y_sort[c]
     x_mine[mine] = x_sort[mine]
@@ -213,35 +215,46 @@
     x_all[y, c] = x_mine[...]
     for j in (0, 1, 3, 2):
         ring_forward(j)
-    xyc.arrived(0, x_half(down, c, 0))
-    xyc.start(4, x_half(down, c, 0), x_half(down, c, 0), device(x, up, z, c))
-    xyc.arrived(1, x_half(up, c, 1))
-    xyc.start(5, x_half(up, c, 1), x_half(up, c, 1), device(x, down, z, c))
-    for h in range(2):
-        for j in (2, 3):
-            wc.arrived(6 + h * 8 + j * 2, w_all.at[h, block(h, -j, -1)])
-        for j in (0, 1):
-            wc.arrived(6 + h * 8 + j * 2 + 1, w_all.at[h, block(h, -j, 1)])
-        for j in range(4):
-            wc.arrived(22 + h * 4 + j, w_all.at[h, block(h, -j, 2)])
     yc.arrived(2, y_all.at[up, 0])
     yc.arrived(3, y_all.at[down, 1])
     yc.arrived(4, y_all.at[y, twin])
     yc.arrived(5, y_all.at[at(y, 2), 0])
     yc.arrived(6, y_all.at[at(y, 2), 1])
 
-    part = jnp.zeros((192, 256), F32)
-    for s in range(4):
-        for h in range(2):
-            part += jnp.dot(
-                y_all[s, :, :, h * 512 : h * 512 + 512].reshape(192, 512),
-                w_all[h, 4 * s : 4 * s + 4].reshape(512, 256),
-                preferred_element_type=F32,
+    def product(j):
+        for h in range(2):
+            if j in (2, 3):
+                wc.arrived(6 + h * 8 + j * 2, w_all.at[h, block(h, -j, -1)])
+            else:
+                wc.arrived(6 + h * 8 + j * 2 + 1, w_all.at[h, block(h, -j, 1)])
+            wc.arrived(22 + h * 4 + j, w_all.at[h, block(h, -j, 2)])
+        s = at(x, -j)
+        total = jnp.dot(
+            y_all[s, :, :, :512].reshape(192, 512),
+            w_all[0, pl.ds(4 * s, 4)].reshape(512, 256),
+            preferred_element_type=F32,
+        )
+        zz = at(z, -j)
+        columns = pl.ds(pl.multiple_of(512 + zz * 128, 128), 128)
+        for s in range(4):
+            total += jnp.dot(
+                y_all[s, :, :, columns].reshape(192, 128), w_all[1, s * 4 + zz], preferred_element_type=F32
             )
+        return total
+
+    part = product(0)
+    part += product(1)
+    xyc.arrived(0, x_half(down, c, 0))
+    xyc.start(4, x_half(down, c, 0), x_half(down, c, 0), device(x, up, z, c))
+    xyc.arrived(1, x_half(up, c, 1))
+    xyc.start(5, x_half(up, c, 1), x_half(up, c, 1), device(x, down, z, c))
+    part += product(3)
+    part += product(2)
     b_part[0] = part[:, :128]
     b_part[1] = part[:, 128:]
     pc.start(0, b_part.at[twin], b_other, device(x, y, z, twin))
     pc.arrived(0, b_other)
+    pl.semaphore_wait(twin_sem, 1)
     for h in range(2):
         keep(b_code.at[h, mine], b_part[c, h * 96 : h * 96 + 96] + b_other[h * 96 : h * 96 + 96])
     gather_first(bc, b_code)
@@ -313,7 +326,7 @@
         lanes = slice(2 * s, 2 * s + 2)
         rows = x_full[0, at(x, d), lanes] if h == 0 else x_full[1, lanes, at(z, d)]
         wide = jnp.dot(rows.reshape(192, 512), u_pair[...], preferred_element_type=F32)
-        value = (wide[:, :128] + wide[:, 128:]).reshape(2, 96, 128)
+        value = wide[:, :128] + wide[:, 128:]
         if d == 0:
             v_own[h, s] = value
         else:
@@ -343,7 +356,7 @@
 
     def use_v(h, s, d):
         along_place = at(x if h == 0 else z, -d)
-        value = decode(v_code.at[h, along_place, 2 * s : 2 * s + 2])
+        value = decode(v_code.at[h, along_place, s]).reshape(2, 96, 128)
         for k in range(2):
             lane = 2 * s + k
             place = along_place * 4 + lane if h == 0 else lane * 4 + along_place
@@ -356,7 +369,7 @@
             for d in (1, 3, 2):
                 vc.arrived(12 + h * 6 + s * 3 + d - 1, v_line.at[h, s, d - 1])
                 total += decode(v_line.at[h, s, d - 1])
-            mine_here = v_code.at[h, x if h == 0 else z, 2 * s : 2 * s + 2]
+            mine_here = v_code.at[h, x if h == 0 else z, s]
             keep(mine_here, total)
             for d in (1, 3, 2):
                 vc.start(24 + h * 6 + s * 3 + d - 1, mine_here, mine_here, along(h, d))
@@ -364,9 +377,7 @@
     for s in range(2):
         for h in range(2):
             for d in (1, 3, 2):
-                vc.arrived(
-                    24 + h * 6 + s * 3 + d - 1, v_code.at[h, at(x if h == 0 else z, -d), 2 * s : 2 * s + 2]
-                )
+                vc.arrived(24 + h * 6 + s * 3 + d - 1, v_code.at[h, at(x if h == 0 else z, -d), s])
                 use_v(h, s, d)
 
     bv = sum(dots)
@@ -383,11 +394,11 @@
     beta = norm / bb
     wide = jnp.dot(x_flip[...], b_pair[...].reshape(TOKENS, 256), preferred_element_type=F32)
     turned = wide[:, :128] + wide[:, 128:] + beta * u0[...].reshape(512, 128)
-    keep(d_code, turned.reshape(4, 128, 128))
     gamma[c, mine] = jnp.broadcast_to(jnp.sum(turned * turned, axis=0, keepdims=True), (8, 128))
     spread = [(dx, dz, e) for dx in (2, 1, 3, 0) for dz in (2, 1, 3, 0) for e in (0, 1) if dx or dz or e]
     for k, (dx, dz, e) in enumerate(spread):
         gc.start(k, gamma.at[c, mine], gamma.at[c, mine], device(at(x, dx), y, at(z, dz), lax.rem(c + e, 2)))
+    keep(d_code, turned.reshape(4, 128, 128))
     hand_over(dc, d_code, d_in)
     dd = jnp.zeros((1, 128), F32)
     for h in range(2):
@@ -442,12 +453,12 @@
         ((512, 256), BF16),
         ((4, 144, 128), BF16),
         ((4, 144, 128), BF16),
-        ((2, 2, 2, 96, 128), F32),
-        ((2, 2, 3, 2, 112, 128), BF16),
-        ((2, 2, 3, 2, 112, 128), BF16),
-        ((2, 2, 2, 112, 128), BF16),
-        ((2, 2, 3, 2, 112, 128), BF16),
-        ((2, 4, 4, 112, 128), BF16),
+        ((2, 2, 192, 128), F32),
+        ((2, 2, 3, 208, 128), BF16),
+        ((2, 2, 3, 208, 128), BF16),
+        ((2, 2, 208, 128), BF16),
+        ((2, 2, 3, 208, 128), BF16),
+        ((2, 4, 2, 208, 128), BF16),
         ((2, 16, 96, 128), F32),
         ((2, 1536, 128), F32),
         ((2, 16, 8, 128), F32),
@@ -461,7 +472,8 @@
         out_shape=jax.ShapeDtypeStruct((256, 256), F32),
         in_specs=[pl.BlockSpec(memory_space=pl.ANY)] * 3,
         out_specs=pl.BlockSpec(memory_space=pltpu.VMEM),
-        scratch_shapes=[pltpu.VMEM(*b) for b in buffers] + [dma((34,))] + [dma((n,)) for n in counts for _ in range(2)],
+        scratch_shapes=[pltpu.VMEM(*b) for b in buffers] + [dma((34,))] + [dma((n,)) for n in counts for _ in range(2)]
+        + [pltpu.SemaphoreType.REGULAR] * 2,
         compiler_params=pltpu.CompilerParams(collective_id=0, has_side_effects=True, vmem_limit_bytes=56 * 2**20),
     )(activations, targets, key_weight)
 

time: 76.1 us -> 74.9 us (0.984)
  Pallas kernels: 74.2 us -> 73 us
    pallas_call x1, Pallas kernels: 74.2 us -> 73 us  [local(): pl.pallas_call(kernel, out_shape=jax.ShapeDtypeStruct((256, 256), F32), i...]
where the time goes in v5:
time: 74.9 us; the launch traced here: 74.7 us
  Pallas kernels  73 us (97%)
  local copies, waits for them, and re-layouts  1.67 us (2%)
    pallas_call x1, Pallas kernels, local(): pl.pallas_call(kernel, out_shape=jax.ShapeDtypeStruct((256, 256), F32), i...  73 us
    unnamed x1, local copies, waits for them, and re-layouts  1.67 us

profile of v5, /device:TPU:1, one launch (start us, length us, event | category | flops | bytes accessed | tf_op | source)
XLA Modules:
  0.0 74.7 jit_solution(16836737911431827073)
XLA Ops:
  0.0 73.0 %shard_map.37 = f32[256,256]{1,0:T(8,128)} custom-call(bf16[96,2048]{1,0:T(8,128)(2,1)} %x_in.1, bf16[96,2048]{1,0:T(8,128)(2,1)} %y_in.1, bf16[256,256]{1,0:T(8,128)(2,1)} %w_in.1), custom_call_target="tpu_custom_call" | custom-call | tf_op jit(solution)/shard_map/pallas_call | solution.py:470
  73.0 1.7 %copy.5 = f32[256,256]{1,0:T(8,128)} copy(f32[256,256]{1,0:T(8,128)} %shard_map.37) | data formatting | bytes 524288

commit v6 on v5

--- a/solution.py
+++ b/solution.py
@@ -153,15 +153,15 @@
             gather_heavy(copies, buf, j)
         for h in range(2):
             for j in (0, 1, 3, 2):
-                use(h, block(h, -j, 0))
-
-    def gather_last(copies, buf, use):
+                use(h, j, 0)
+
+    def gather_last(copies, buf, use, done):
         for j in (0, 1, 3, 2):
             for h in range(2):
                 for d in (1, 3, 2):
-                    place = block(h, -j, -d)
-                    copies.arrived(6 + h * 12 + j * 3 + d - 1, buf.at[h, place])
-                    use(h, place)
+                    copies.arrived(6 + h * 12 + j * 3 + d - 1, buf.at[h, block(h, -j, -d)])
+                    use(h, j, d)
+                done(h, j)
 
     def ring_heavy(j):
         for h in range(2):
@@ -252,49 +252,64 @@
     part += product(2)
     b_part[0] = part[:, :128]
     b_part[1] = part[:, 128:]
-    pc.start(0, b_part.at[twin], b_other, device(x, y, z, twin))
-    pc.arrived(0, b_other)
+    for h in range(2):
+        rows = slice(h * 96, h * 96 + 96)
+        pc.start(h, b_part.at[twin, rows], b_other.at[rows], device(x, y, z, twin))
     pl.semaphore_wait(twin_sem, 1)
     for h in range(2):
+        pc.arrived(h, b_other.at[h * 96 : h * 96 + 96])
         keep(b_code.at[h, mine], b_part[c, h * 96 : h * 96 + 96] + b_other[h * 96 : h * 96 + 96])
     gather_first(bc, b_code)
 
     norms = []
 
-    def use_b(h, place):
-        value = decode(b_code.at[h, place])
+    first_axis, second_axis = (x, z), (z, x)
+    wide = [jnp.zeros((512, 256), F32)]
+
+    def accumulate(h, j):
+        group = at(first_axis[h], -j)
+        tokens = pl.ds(pl.multiple_of(h * 1536 + group * 384, 128), 384)
+        wide[0] += jnp.dot(
+            x_flip[:, tokens], b_pair[h, pl.ds(group * 4, 4)].reshape(384, 256), preferred_element_type=F32
+        )
+
+    def use_b(h, j, d):
+        place = at(first_axis[h], -j) * 4 + at(second_axis[h], -d)
+        value = decode(b_code.at[h, block(h, -j, -d)])
         b_all[h, place] = value
         norms.append(jnp.sum(value * value, axis=0, keepdims=True))
         high, low = split(value)
         b_pair[h, place, :, :128] = high
         b_pair[h, place, :, 128:] = low
 
-    gather_rest(bc, b_code, use_b)
+    def arrange(s, e):
+        piece = x_all[s, e].reshape(1536, 128)
+        columns = pl.ds(pl.multiple_of(s * 128, 128), 128)
+        x_full[e, :, :, :, columns] = piece.reshape(4, 4, 96, 128)
+        for m in range(4):
+            group = [x_all[s, e, m * 4 + k + 3 * e * (k - m)] for k in range(4)]
+            tokens = pl.ds(pl.multiple_of(e * 1536 + m * 384, 128), 384)
+            x_flip[columns, tokens] = jnp.concatenate(group, axis=0).T
+
     xyc.arrived(2, x_half(up, c, 0))
     xcc.start(3, x_all.at[up, c], x_all.at[up, c], device(x, y, z, twin))
     xyc.arrived(3, x_half(down, c, 1))
     xcc.start(1, x_all.at[down, c], x_all.at[down, c], device(x, y, z, twin))
+    for s in (y, up, down):
+        arrange(s, c)
+    gather_rest(bc, b_code, use_b)
     xyc.arrived(4, x_half(at(y, 2), c, 0))
     xyc.arrived(5, x_half(at(y, 2), c, 1))
     xcc.start(2, x_all.at[at(y, 2), c], x_all.at[at(y, 2), c], device(x, y, z, twin))
-
-    def arrange(s, e):
-        piece = x_all[s, e].reshape(1536, 128)
-        columns = pl.ds(pl.multiple_of(s * 128, 128), 128)
-        rows = pl.ds(pl.multiple_of(e * 1536, 128), 1536)
-        x_full[e, :, :, :, columns] = piece.reshape(4, 4, 96, 128)
-        x_flip[columns, rows] = piece.T
-
-    for d in (0, 1, 3, 2):
-        arrange(at(y, -d), c)
-    for d in (0, 1, 3, 2):
+    arrange(at(y, 2), c)
+    for d in (0, 3, 1, 2):
         xcc.arrived(d, x_all.at[at(y, -d), twin])
         arrange(at(y, -d), twin)
 
-    gather_last(bc, b_code, use_b)
+    gather_last(bc, b_code, use_b, accumulate)
     bb = sum(norms)
-    wide = jnp.dot(x_flip[...], b_pair[...].reshape(TOKENS, 256), preferred_element_type=F32)
-    first = wide[:, :128] + wide[:, 128:]
+    first = wide[0][:, :128] + wide[0][:, 128:]
+    wide[0] = jnp.zeros((512, 256), F32)
     u0[...] = first.reshape(4, 128, 128)
     high, low = split(first * (1.0 / TOKENS))
     u_pair[:, :128] = high
@@ -325,8 +340,8 @@
     def multiply(h, s, d):
         lanes = slice(2 * s, 2 * s + 2)
         rows = x_full[0, at(x, d), lanes] if h == 0 else x_full[1, lanes, at(z, d)]
-        wide = jnp.dot(rows.reshape(192, 512), u_pair[...], preferred_element_type=F32)
-        value = wide[:, :128] + wide[:, 128:]
+        both = jnp.dot(rows.reshape(192, 512), u_pair[...], preferred_element_type=F32)
+        value = both[:, :128] + both[:, 128:]
         if d == 0:
             v_own[h, s] = value
         else:
@@ -358,10 +373,14 @@
         along_place = at(x if h == 0 else z, -d)
         value = decode(v_code.at[h, along_place, s]).reshape(2, 96, 128)
         for k in range(2):
-            lane = 2 * s + k
-            place = along_place * 4 + lane if h == 0 else lane * 4 + along_place
+            place = along_place * 4 + 2 * s + k
             v_all[h, place] = value[k]
             dots.append(jnp.sum(value[k] * b_all[h, place], axis=0, keepdims=True))
+            high, low = split(value[k])
+            b_pair[h, place, :, :128] = high
+            b_pair[h, place, :, 128:] = low
+        if s == 1:
+            accumulate(h, d)
 
     for s in range(2):
         for h in range(2):
@@ -388,12 +407,8 @@
         residual = value - alpha * (v_all[h].reshape(1536, 128) + RIDGE * value)
         norm += jnp.sum(residual * residual, axis=0, keepdims=True)
         r_all[h] = residual
-        high, low = split(residual)
-        b_pair[h, :, :, :128] = high.reshape(16, 96, 128)
-        b_pair[h, :, :, 128:] = low.reshape(16, 96, 128)
     beta = norm / bb
-    wide = jnp.dot(x_flip[...], b_pair[...].reshape(TOKENS, 256), preferred_element_type=F32)
-    turned = wide[:, :128] + wide[:, 128:] + beta * u0[...].reshape(512, 128)
+    turned = (1.0 - RIDGE * alpha + beta) * u0[...].reshape(512, 128) - alpha * (wide[0][:, :128] + wide[0][:, 128:])
     gamma[c, mine] = jnp.broadcast_to(jnp.sum(turned * turned, axis=0, keepdims=True), (8, 128))
     spread = [(dx, dz, e) for dx in (2, 1, 3, 0) for dz in (2, 1, 3, 0) for e in (0, 1) if dx or dz or e]
     for k, (dx, dz, e) in enumerate(spread):
@@ -466,7 +481,7 @@
         ((4, 144, 128), BF16),
         ((4, 144, 128), BF16),
     ]
-    counts = (7, 30, 15, 6, 4, 1, 30, 36, 31, 1, 4, 4)
+    counts = (7, 30, 15, 6, 4, 2, 30, 36, 31, 1, 4, 4)
     return pl.pallas_call(
         kernel,
         out_shape=jax.ShapeDtypeStruct((256, 256), F32),

time: 74.9 us -> 74.3 us (level)
  no operation moved by 1% of the time
where the time goes in v6:
time: 74.3 us; the launch traced here: 74.1 us
  Pallas kernels  72.4 us (97%)
  local copies, waits for them, and re-layouts  1.67 us (2%)
    pallas_call x1, Pallas kernels, local(): pl.pallas_call(kernel, out_shape=jax.ShapeDtypeStruct((256, 256), F32), i...  72.4 us
    unnamed x1, local copies, waits for them, and re-layouts  1.67 us

profile of v6, /device:TPU:1, one launch (start us, length us, event | category | flops | bytes accessed | tf_op | source)
XLA Modules:
  0.0 74.1 jit_solution(7001343746743947117)
XLA Ops:
  0.0 72.4 %shard_map.37 = f32[256,256]{1,0:T(8,128)} custom-call(bf16[96,2048]{1,0:T(8,128)(2,1)} %x_in.1, bf16[96,2048]{1,0:T(8,128)(2,1)} %y_in.1, bf16[256,256]{1,0:T(8,128)(2,1)} %w_in.1), custom_call_target="tpu_custom_call" | custom-call | tf_op jit(solution)/shard_map/pallas_call | solution.py:485
  72.4 1.7 %copy.5 = f32[256,256]{1,0:T(8,128)} copy(f32[256,256]{1,0:T(8,128)} %shard_map.37) | data formatting | bytes 524288
